TPU v7x, 256 devices: a whole 4x4x8 slice. The times are simulated.
256 devices in a mesh: dp: 16 (over z, core), tensor: 16 (over y, x).
Axes of the slice: x: 4, y: 4, z: 8, core: 2. Of those that a mesh axis runs over, the one named last changes fastest.
Arguments:
- gate_act: bfloat16 [6144, 14336], P('dp', 'tensor'), may hold values from -6 to 6
- up_act: bfloat16 [6144, 14336], P('dp', 'tensor'), may hold values from -6 to 6
- cotangent: bfloat16 [6144, 4096], P(('dp', 'tensor')), may hold values from -60 to 60
- frozen_weight: bfloat16 [14336, 4096], P('tensor'), may hold values from -1 to 1
- adapter_in: bfloat16 [64, 14336], P(None, 'tensor'), may hold values from -0.046875 to 0.046875
- adapter_out: bfloat16 [64, 4096], replicated, may hold values from -0.75 to 0.75
- magnitude: float32 [4096], replicated, may hold values from 1 to 8
Outputs:
- grad_gate: bfloat16 [6144, 14336], P('dp', 'tensor')
- grad_up: bfloat16 [6144, 14336], P('dp', 'tensor')
- grad_adapter_in: float32 [64, 14336], P(None, 'tensor')
- grad_adapter_out: float32 [64, 4096], replicated
- grad_magnitude: float32 [4096], replicated
All inputs are finite; a program needn't handle non-finite values.
Results may differ from a plain program's by a relative error of at most 0.0075.
Values may be sent and summed in bfloat16 or wider, within the bound.
A program may use at most 128 MiB of HBM per device.

v0:
```python
import jax
import jax.numpy as jnp
from jax import lax
from jax.sharding import PartitionSpec as P

epsilon = 1e-06


def contract(left, right, left_dim, right_dim):
    return lax.dot_general(
        left, right, (((left_dim,), (right_dim,)), ((), ())), preferred_element_type=jnp.float32
    )


def split_product(rows, scaled):
    rows_high = rows.astype(jnp.bfloat16)
    rows_low = (rows - rows_high.astype(jnp.float32)).astype(jnp.bfloat16)
    return contract(rows_high, scaled, 0, 0) + contract(rows_low, scaled, 0, 0)


def on_device(gate_act, up_act, cotangent, frozen_weight, adapter_in, adapter_out, magnitude):
    gate_value = gate_act.astype(jnp.float32)
    up_value = up_act.astype(jnp.float32)
    sigmoid_gate = jax.nn.sigmoid(gate_value)
    hidden = (gate_value * sigmoid_gate * up_value).astype(jnp.bfloat16)
    projected_part = contract(hidden, adapter_in, 1, 1)
    low_rank = contract(adapter_in, adapter_out, 0, 0)
    adjusted = frozen_weight.astype(jnp.float32) + 2.0 * low_rank
    squares = jnp.sum(adjusted * adjusted, axis=0)
    adjusted_low = adjusted.astype(jnp.bfloat16)
    full_cot = lax.all_gather(cotangent, "tensor", axis=0, tiled=True)
    squares = lax.psum(squares, "tensor")
    own_rows = lax.psum_scatter(
        jnp.dot(hidden, adjusted_low, preferred_element_type=jnp.float32),
        "tensor",
        scatter_dimension=0,
        tiled=True,
    )
    magnitude_part = jnp.sum(cotangent.astype(jnp.float32) * own_rows, axis=0)
    magnitude_sum = lax.psum(magnitude_part, ("dp", "tensor"))
    column_norm = jnp.sqrt(squares + epsilon)
    grad_magnitude = magnitude_sum / column_norm
    column_scale = magnitude / column_norm
    scaled = (full_cot.astype(jnp.float32) * column_scale).astype(jnp.bfloat16)
    hidden_grad = contract(scaled, adjusted_low, 1, 1)
    grad_up = (hidden_grad * gate_value * sigmoid_gate).astype(jnp.bfloat16)
    grad_gate = (
        hidden_grad * up_value * sigmoid_gate * (1.0 + gate_value * (1.0 - sigmoid_gate))
    ).astype(jnp.bfloat16)
    rank_cot = contract(scaled, adapter_out, 1, 1).astype(jnp.bfloat16)
    in_part = contract(rank_cot, hidden, 0, 0)
    out_part = split_product(projected_part, scaled)
    in_sum = lax.psum(in_part, "dp")
    out_sum = lax.psum(out_part, ("dp", "tensor"))
    return (grad_gate, grad_up, 2.0 * in_sum, 2.0 * out_sum, grad_magnitude)


def solution(mesh):
    in_specs = (
        P("dp", "tensor"),
        P("dp", "tensor"),
        P(("dp", "tensor"), None),
        P("tensor", None),
        P(None, "tensor"),
        P(),
        P(),
    )
    out_specs = (P("dp", "tensor"), P("dp", "tensor"), P(None, "tensor"), P(), P())
    return jax.shard_map(
        on_device, mesh=mesh, in_specs=in_specs, out_specs=out_specs, check_vma=False
    )
```

profile of v0, /device:TPU:1, one launch (start us, length us, event | category | flops | bytes accessed | tf_op | source)
XLA Modules:
  0.0 649.5 jit_solution(4446286872400227739)
XLA Ops:
  7.2 0.0 copy-start
  7.2 0.0 all-gather.2.cloned.1.call-start
  7.2 0.7 all-gather.2.cloned.1.call-update
  7.9 0.0 copy-start.3
  7.9 0.0 copy-start.4
  7.9 0.0 copy-start.5
  7.9 0.0 all-reduce.4.cloned.1.call-start
  8.0 0.2 copy-done
  8.2 8.7 %multiply_reduce_fusion = (f32[4096]{0:T(1024)S(1)}, f32[896,4096]{1,0:T(8,128)}) fusion(bf16[896,4096]{1,0:T(8,128)(2,1)} %param.10, bf16[64,896]{1,0:T(8,128)(2,1)} %param.11, bf16[64,4096]{1,0:T(8,128)(2,1)S(1)} %copy-done), kind=kOutput, calls=%fused_computation | convolution fusion | flops 488108032 | bytes 22675456 | tf_op jit(solution)/shard_map/dot_general | solution.py:10
  16.9 61.6 %psum.28 = f32[4096]{0:T(1024)S(1)} all-reduce(f32[4096]{0:T(1024)S(1)} %get-tuple-element.8), channel_id=1, replica_groups=mesh['dp'=16,'tensor'=16] {'tensor'}, use_global_device_ids=true, to_apply=%region_1.0 | all-reduce | flops 4096 | bytes 32768 | tf_op jit(solution)/shard_map/psum | solution.py:32
  78.5 0.0 copy-done.3
  78.5 0.0 all-gather.2.cloned.1.call-done
  78.5 0.0 copy-done.4
  78.5 0.0 copy-done.5
  78.5 0.0 copy-start.2
  78.5 13.3 %fusion.13 = (bf16[384,896]{1,0:T(8,128)(2,1)}, bf16[384,896]{1,0:T(8,128)(2,1)}, bf16[384,896]{1,0:T(8,128)(2,1)S(1)}) fusion(bf16[384,896]{1,0:T(8,128)(2,1)S(1)} %copy-done.4, bf16[384,896]{1,0:T(8,128)(2,1)S(1)} %copy-done.5, f32[896,4096]{1,0:T(8,128)} %get-tuple-element.9, bf16[896,4096]{1,0:T(8,128)(2,1)} %param.10, ...), kind=kOutput, calls=%fused_computation.23 | convolution fusion | flops 2844164096 | bytes 28622848 | tf_op jit(solution)/shard_map/dot_general | solution.py:10
  91.8 0.0 copy-done.2
  91.8 0.3 fusion.23
  92.2 3.9 fusion.15
  96.1 0.0 all-reduce.4.cloned.1.call-update
  96.1 0.0 all-reduce.6.cloned.1.call-start
  96.2 2.7 fusion.1
  98.9 3.7 convolution_add_fusion
  102.5 0.0 all-reduce.6.cloned.1.call-update
  102.6 0.0 reduce-scatter.4.cloned.1.call-start
  102.6 12.7 %fusion.20 = f32[384,4096]{1,0:T(8,128)} fusion(bf16[384,896]{1,0:T(8,128)(2,1)S(1)} %get-tuple-element.7, f32[896,4096]{1,0:T(8,128)} %get-tuple-element.9, bf16[896,4096]{1,0:T(8,128)(2,1)} %param.10), kind=kOutput, calls=%fused_computation.35 | convolution fusion | flops 2833252352 | bytes 28999680 | tf_op jit(solution)/shard_map/dot_general | solution.py:34
  115.3 0.0 copy-start.1
  115.3 0.0 reduce-scatter.4.cloned.1.call-update
  115.3 100.2 %all-reduce.4.cloned.1.call-done = f32[64,896]{1,0:T(8,128)} async-done(((f32[64,896]{1,0:T(8,128)}), f32[64,896]{1,0:T(8,128)}) %all-reduce.4.cloned.1.call-update) | async-done | bytes 229392 | tf_op jit(solution)/shard_map/psum | solution.py:53
  215.5 1.6 broadcast_multiply_fusion.1
  217.1 258.5 %all-reduce.6.cloned.1.call-done = f32[64,4096]{1,0:T(8,128)} async-done(((f32[64,4096]{1,0:T(8,128)}), f32[64,4096]{1,0:T(8,128)}) %all-reduce.6.cloned.1.call-update) | async-done | bytes 1048592 | tf_op jit(solution)/shard_map/psum | solution.py:54
  475.6 2.3 broadcast_multiply_fusion
  477.9 86.8 %reduce-scatter.4.cloned.1.call-done = f32[24,4096]{1,0:T(8,128)} async-done(((f32[384,4096]{1,0:T(8,128)}), f32[24,4096]{1,0:T(8,128)}) %reduce-scatter.4.cloned.1.call-update) | async-done | bytes 393232
  564.6 0.0 copy-done.1
  564.6 1.1 multiply_reduce_fusion.1
  565.7 76.7 %psum.31 = f32[4096]{0:T(1024)S(1)} all-reduce(f32[4096]{0:T(1024)S(1)} %multiply_reduce_fusion.1), channel_id=1, replica_groups=mesh['dp'=16,'tensor'=16] {'dp','tensor'}, use_global_device_ids=true, to_apply=%region_6.0 | all-reduce | flops 4096 | bytes 32768 | tf_op jit(solution)/shard_map/psum | solution.py:40
  642.4 0.6 fusion.18
  (1 shorter events, 0.0 us)
Async XLA Ops:
  7.2 1.0 copy-start
  7.2 71.3 %all-gather.2.cloned.1.call-start = ((), (), s32[]{:S(2)}) async-start(), calls=%async_computation.1 | async-start | bytes 3342336 | tf_op jit(solution)/shard_map/all_gather | solution.py:31
  7.9 70.6 %copy-start.3 = (f32[4096]{0:T(1024)S(1)}, f32[4096]{0:T(1024)}, u32[]{:S(2)}) copy-start(f32[4096]{0:T(1024)} %param.13) | copy-start | bytes 49156
  7.9 70.6 %copy-start.4 = (bf16[384,896]{1,0:T(8,128)(2,1)S(1)}, bf16[384,896]{1,0:T(8,128)(2,1)}, u32[]{:S(2)}) copy-start(bf16[384,896]{1,0:T(8,128)(2,1)} %param.7) | copy-start | bytes 2064388
  7.9 70.6 %copy-start.5 = (bf16[384,896]{1,0:T(8,128)(2,1)S(1)}, bf16[384,896]{1,0:T(8,128)(2,1)}, u32[]{:S(2)}) copy-start(bf16[384,896]{1,0:T(8,128)(2,1)} %param.8) | copy-start | bytes 2064388
  7.9 207.5 %all-reduce.4.cloned.1.call-start = ((), (), s32[]{:S(2)}) async-start(), calls=%async_computation.2 | async-start | bytes 458752 | tf_op jit(solution)/shard_map/psum | solution.py:53
  78.5 13.3 %copy-start.2 = (bf16[64,896]{1,0:T(8,128)(2,1)S(1)}, bf16[64,896]{1,0:T(8,128)(2,1)}, u32[]{:S(2)}) copy-start(bf16[64,896]{1,0:T(8,128)(2,1)} %param.11) | copy-start | bytes 344068
  96.1 379.5 %all-reduce.6.cloned.1.call-start = ((), (), s32[]{:S(2)}) async-start(), calls=%async_computation.3 | async-start | bytes 2097152 | tf_op jit(solution)/shard_map/psum | solution.py:54
  102.6 462.1 %reduce-scatter.4.cloned.1.call-start = ((), (), s32[]{:S(2)}) async-start(), calls=%async_computation.4 | async-start | bytes 6684672
  115.3 449.3 %copy-start.1 = (bf16[24,4096]{1,0:T(8,128)(2,1)S(1)}, bf16[24,4096]{1,0:T(8,128)(2,1)}, u32[]{:S(2)}) copy-start(bf16[24,4096]{1,0:T(8,128)(2,1)} %param.9) | copy-start | bytes 589828
Sparse Core Ops, SparseCore 0:
  10.4 56.5 all-gather.1
  96.2 119.1 all-reduce.3
  222.4 253.1 all-reduce.5
  479.2 85.4 reduce-scatter.3
where the time goes:
time: 650 us
  waiting for transfers between devices  446 us (69%)
  blocking collectives  138 us (21%)
  matrix products  45.3 us (7%)
  between operations  13.8 us (2%)
    psum x1, waiting for transfers between devices, on_device(): out_sum = lax.psum(out_part, ('dp', 'tensor'))  258 us
    psum x1, waiting for transfers between devices, on_device(): in_sum = lax.psum(in_part, 'dp')  100 us
    unnamed x5, waiting for transfers between devices  87.5 us
    psum x1, blocking collectives, on_device(): magnitude_sum = lax.psum(magnitude_part, ('dp', 'tensor'))  76.7 us
    psum x1, blocking collectives, on_device(): squares = lax.psum(squares, 'tensor')  61.6 us
    dot_general x6, matrix products, contract(): lax.dot_general(left, right, (((left_dim,), (right_dim,)), ((), ())), pre...  32.6 us
  transfers between devices with their start and end apart: 4, of which 3 were waited for; matrix products, arithmetic and copies ran while one was open for 5% of the time, Pallas kernels for 0%

commit v1 on v0

v1 whole, which is shorter than its diff:
```python
import jax
import jax.numpy as jnp
from jax import lax
from jax.experimental import pallas as pl
from jax.experimental.pallas import tpu as pltpu
from jax.sharding import PartitionSpec as P

epsilon = 1e-06
MESH = pl.DeviceIdType.MESH
f32 = jnp.float32
bf16 = jnp.bfloat16

LINE = 4
PEERS = LINE * LINE
GROUP = 16
DEPTH = GROUP // 2
ROWS = 24
TOK = ROWS * PEERS
F = 896
D = 4096
RANK = 64
HALF = D // 2
QUART = D // 4
COLS = D // PEERS
WBLK = 128
NWB = F // WBLK

(J, SQ_RS, SQ_AG, PR_RS, PR_AG, RC_AG, IN_RS, IN_AG, O_RS, O_PL, O_Z, O_CORE, M_RS, M_DP, M_AG) = range(15)
N_PHASES = 15


def dot(a, b, da, db):
    return lax.dot_general(a, b, (((da,), (db,)), ((), ())), preferred_element_type=f32)


def kernel(
    gate_h, up_h, cot_h, w_h, ain_h, aout_h, mag_h,
    ggate_h, gup_h, gin_h, gout_h, gmag_h,
    w_v, gate_v, up_v, hid_v, u_v, v_v, cot_v, ain_v, aout_v, mag_v, aint_v,
    cotb, scaled, prod, hg, sqacc, magacc, scale_v, norm_v,
    jsend, jrecv, sjv, sqp, sqr, sqf, prs, prr, pra, rcs, rca, lv,
    ipart, irecv, isum, iag, gin_v, opart, orecv, opl, ob, gout_v,
    magp, magr, magd, gmag_v, out_a, out_b,
    loc_sem, w_sem, out_sem, ph_send, ph_recv, g_send, g_recv,
):
    me_t = lax.axis_index("tensor")
    me_d = lax.axis_index("dp")
    x = lax.rem(me_t, LINE)
    y = lax.div(me_t, LINE)
    z = lax.div(me_d, 2)
    core = lax.rem(me_d, 2)

    loads = [
        pltpu.make_async_copy(cot_h, cot_v, loc_sem.at[0]),
        pltpu.make_async_copy(gate_h, gate_v, loc_sem.at[1]),
        pltpu.make_async_copy(up_h, up_v, loc_sem.at[2]),
        pltpu.make_async_copy(ain_h, ain_v.at[pl.ds(0, RANK)], loc_sem.at[3]),
        pltpu.make_async_copy(ain_h, ain_v.at[pl.ds(RANK, RANK)], loc_sem.at[4]),
        pltpu.make_async_copy(aout_h, aout_v.at[pl.ds(0, RANK)], loc_sem.at[5]),
        pltpu.make_async_copy(aout_h, aout_v.at[pl.ds(RANK, RANK)], loc_sem.at[6]),
        pltpu.make_async_copy(mag_h, mag_v, loc_sem.at[7]),
    ]
    for c in loads:
        c.start()

    def w_copy(i):
        rows = pl.ds(pl.multiple_of(i * WBLK, WBLK), WBLK)
        return pltpu.make_async_copy(w_h.at[rows], w_v.at[rows], w_sem.at[i])

    for i in range(NWB):
        w_copy(i).start()

    barrier = pltpu.get_barrier_semaphore()

    @pl.loop(1, PEERS)
    def _(d):
        pl.semaphore_signal(barrier, inc=1, device_id={"tensor": lax.rem(me_t + d, PEERS)}, device_id_type=MESH)

    @pl.loop(1, GROUP)
    def _(d):
        pl.semaphore_signal(barrier, inc=1, device_id={"dp": lax.rem(me_d + d, GROUP)}, device_id_type=MESH)

    loads[0].wait()
    for h in range(2):
        left = cot_v[:, HALF * h : HALF * h + QUART].astype(f32)
        right = cot_v[:, HALF * h + QUART : HALF * (h + 1)].astype(f32)
        cotb[h, me_t] = jnp.concatenate([left, right], axis=0).astype(bf16)
    for t in range(PEERS):
        left = cot_v[:, COLS * t : COLS * t + 128].astype(f32)
        right = cot_v[:, COLS * t + 128 : COLS * (t + 1)].astype(f32)
        jsend[t] = jnp.concatenate([left, right], axis=0).astype(bf16)
    jrecv[me_t] = jsend[me_t]

    pl.semaphore_wait(barrier, PEERS + GROUP - 2)

    def slot(h, along, across):
        if h == 0:
            return lax.rem(y + across + LINE, LINE) * LINE + lax.rem(x + along + LINE, LINE)
        return lax.rem(y + along + LINE, LINE) * LINE + lax.rem(x + across + LINE, LINE)

    def move(h, along, across, part, to, sem):
        if part is None:
            ref = cotb.at[h, slot(h, along, across)]
        else:
            ref = cotb.at[h, slot(h, along, across), :, pl.ds(part * (QUART // 2), QUART // 2)]
        return pltpu.make_async_remote_copy(
            src_ref=ref, dst_ref=ref, send_sem=g_send.at[20 * h + sem], recv_sem=g_recv.at[20 * h + sem],
            device_id={"tensor": to}, device_id_type=MESH,
        )

    sent = []

    def go(h, along, across, part, to, sem):
        c = move(h, along, across, part, to, sem)
        c.start()
        sent.append(c)

    def arrive(h, along, across, part, sem):
        move(h, along, across, part, slot(h, 0, 1), sem).wait_recv()

    offsets = (0, -1, 1, 2)

    def send_across(h, j):
        go(h, offsets[j], 0, None, slot(h, 0, 1), 4 + 4 * j)
        go(h, offsets[j], 0, None, slot(h, 0, -1), 5 + 4 * j)

    def forward_across(h, j):
        arrive(h, offsets[j], -1, None, 4 + 4 * j)
        go(h, offsets[j], -1, 0, slot(h, 0, 1), 6 + 4 * j)
        arrive(h, offsets[j], 1, None, 5 + 4 * j)
        go(h, offsets[j], 1, 1, slot(h, 0, -1), 7 + 4 * j)

    def last_across(h, j):
        arrive(h, offsets[j], 2, 0, 6 + 4 * j)
        arrive(h, offsets[j], 2, 1, 7 + 4 * j)

    for h in range(2):
        go(h, 0, 0, None, slot(h, 1, 0), 0)
        go(h, 0, 0, None, slot(h, -1, 0), 1)
    for h in range(2):
        send_across(h, 0)

    def exchange(phase, axis, src, dst, me, n):
        def one(p):
            return pltpu.make_async_remote_copy(
                src_ref=src(p), dst_ref=dst, send_sem=ph_send.at[phase], recv_sem=ph_recv.at[phase],
                device_id={axis: p}, device_id_type=MESH,
            )

        @pl.loop(1, n)
        def _(d):
            one(lax.rem(me + d, n)).start()

    def got(phase, ref):
        pltpu.make_async_copy(ref, ref, ph_recv.at[phase]).wait()

    def left_here(phase, ref):
        pltpu.make_async_copy(ref, ref, ph_send.at[phase]).wait()

    def to_plane(phase, src, dst):
        exchange(phase, "tensor", src, dst, me_t, PEERS)

    def to_group(phase, src, dst):
        exchange(phase, "dp", src, dst, me_d, GROUP)

    def my_cols(p):
        return pl.ds(pl.multiple_of(p * COLS, COLS), COLS)

    fifteen = pl.ds(0, 15)
    fifteen_cols = pl.ds(0, 15 * COLS)

    to_plane(J, lambda p: jsend.at[p], jrecv.at[me_t])

    loads[1].wait()
    loads[2].wait()

    @pl.loop(0, TOK // 16)
    def _(i):
        rows = pl.ds(pl.multiple_of(i * 16, 16), 16)
        g = gate_v[rows, :].astype(f32)
        u = up_v[rows, :].astype(f32)
        s = 1.0 / (1.0 + jnp.exp(-g))
        gs = g * s
        hid_v[rows, :] = (gs * u).astype(bf16)
        u_v[rows, :] = gs
        v_v[rows, :] = u * s * (1.0 + g * (1.0 - s))

    loads[3].wait()
    loads[4].wait()
    low_lanes = lax.broadcasted_iota(jnp.int32, (8, 128), 1) < RANK
    part = dot(hid_v[...], ain_v[...], 1, 1)
    for t in range(PEERS):
        r = ROWS * t
        prs[t, 0:8] = jnp.where(low_lanes, part[r : r + 8], part[r + 8 : r + 16])
        prs[t, 8:16] = part[r + 16 : r + 24]
    prr[me_t] = prs[me_t]
    to_plane(PR_RS, lambda p: prs.at[p], prr.at[me_t])

    aint_v[...] = (2.0 * jnp.transpose(ain_v[0:RANK, :].astype(f32), (1, 0))).astype(bf16)
    loads[5].wait()
    loads[6].wait()
    sqacc[...] = jnp.zeros_like(sqacc)

    def adjust(i):
        w_copy(i).wait()
        rows = pl.ds(pl.multiple_of(i * WBLK, WBLK), WBLK)
        lhs = aint_v[rows, :]
        for c in range(8):
            cols = slice(512 * c, 512 * (c + 1))
            a = w_v[rows, cols].astype(f32) + dot(lhs, aout_v[0:RANK, cols], 1, 0)
            w_v[rows, cols] = a.astype(bf16)
            sqacc[:, cols] += jnp.sum((a * a).reshape(WBLK // 8, 8, 512), axis=0)

    pl.loop(0, 4)(adjust)

    for h in range(2):
        arrive(h, -1, 0, None, 0)
        go(h, -1, 0, 0, slot(h, 1, 0), 2)
        arrive(h, 1, 0, None, 1)
        go(h, 1, 0, 1, slot(h, -1, 0), 3)
    for h in range(2):
        send_across(h, 1)
        send_across(h, 2)

    pl.loop(4, NWB)(adjust)

    sqp[...] = jnp.sum(sqacc[...], axis=0, keepdims=True)
    sqr[me_t] = sqp[:, my_cols(me_t)]
    to_plane(SQ_RS, lambda p: sqp.at[:, my_cols(p)], sqr.at[me_t])

    for h in range(2):
        forward_across(h, 0)

    got(PR_RS, prr.at[fifteen])
    total = prr[0]
    for t in range(1, PEERS):
        total = total + prr[t]
    pra[me_t] = total
    to_plane(PR_AG, lambda p: pra.at[me_t], pra.at[me_t])

    def produce(i):
        cols = pl.ds(pl.multiple_of(i * 256, 256), 256)
        prod[:, cols] = dot(hid_v[...], w_v[:, cols], 1, 0)

    pl.loop(0, 6)(produce)

    got(SQ_RS, sqr.at[fifteen])
    total = sqr[0]
    for t in range(1, PEERS):
        total = total + sqr[t]
    sqf[:, my_cols(me_t)] = total
    to_plane(SQ_AG, lambda p: sqf.at[:, my_cols(me_t)], sqf.at[:, my_cols(me_t)])

    for h in range(2):
        arrive(h, 2, 0, 0, 2)
        arrive(h, 2, 0, 1, 3)
        send_across(h, 3)

    pl.loop(6, 16)(produce)

    for h in range(2):
        forward_across(h, 1)
        forward_across(h, 2)

    loads[7].wait()
    got(SQ_AG, sqf.at[:, fifteen_cols])
    norm_v[...] = jnp.sqrt(sqf[...] + epsilon)
    scale_v[...] = mag_v[...] / norm_v[...]

    rank = jnp.zeros((32, 128), f32)
    for c in range(8):
        cols = slice(512 * c, 512 * (c + 1))
        s = cot_v[:, cols].astype(f32) * scale_v[:, cols]
        s = jnp.concatenate([s, jnp.zeros((8, 512), f32)], axis=0).astype(bf16)
        rank = rank + dot(s, aout_v[:, cols], 1, 1)
    rcs[...] = jnp.concatenate([jnp.where(low_lanes, rank[0:8], rank[8:16]), rank[16:24]], axis=0).astype(bf16)
    rca[me_t] = rcs[...]
    to_plane(RC_AG, lambda p: rcs, rca.at[me_t])

    got(J, jrecv.at[fifteen])
    got(PR_AG, pra.at[fifteen])
    scale_j = scale_v[:, my_cols(me_t)]
    for t in range(0, PEERS, 2):
        c0 = jrecv[t].astype(f32)
        c1 = jrecv[t + 1].astype(f32)
        left = jnp.concatenate([c0[0:24], c1[0:24]], axis=0) * scale_j[:, 0:128]
        right = jnp.concatenate([c0[24:48], c1[24:48]], axis=0) * scale_j[:, 128:256]
        sjv[ROWS * t : ROWS * (t + 2), 0:128] = left.astype(bf16)
        sjv[ROWS * t : ROWS * (t + 2), 128:256] = right.astype(bf16)

        def both(tile, last):
            turned = pltpu.roll(tile, RANK, 1)
            return [jnp.where(low_lanes, tile, turned), jnp.where(low_lanes, turned, tile), last]

        rows = jnp.concatenate(
            both(pra[t, 0:8], pra[t, 8:16]) + both(pra[t + 1, 0:8], pra[t + 1, 8:16]), axis=0
        )
        high = rows.astype(bf16).astype(f32)
        lanes = lax.broadcasted_iota(jnp.int32, rows.shape, 1) < RANK
        lv[ROWS * t : ROWS * (t + 2), :] = jnp.where(lanes, high, rows - high).astype(bf16)
    o = dot(lv[...], sjv[...], 0, 0)
    o = o[0:RANK] + o[RANK:]
    for p in range(GROUP):
        opart[p] = o[8 * (p // 2) : 8 * (p // 2) + 8, 128 * (p % 2) : 128 * (p % 2) + 128]
    orecv[me_d] = opart[me_d]
    to_group(O_RS, lambda p: opart.at[p], orecv.at[me_d])

    for h in range(2):
        forward_across(h, 3)

    got(RC_AG, rca.at[fifteen])
    for t in range(0, PEERS, 2):
        c0 = rca[t].astype(f32)
        c1 = rca[t + 1].astype(f32)
        rows = jnp.concatenate(
            [c0[0:8], pltpu.roll(c0[0:8], RANK, 1), c0[8:16], c1[0:8], pltpu.roll(c1[0:8], RANK, 1), c1[8:16]], axis=0
        )
        lv[ROWS * t : ROWS * (t + 2), :] = rows.astype(bf16)
    for g in range(4):
        w = 256 if g < 3 else 128
        o = dot(lv[...], hid_v[:, 256 * g : 256 * g + w], 0, 0)
        for b in range(4):
            ipart[4 * b + g, :, 0:w] = o[16 * b : 16 * b + 16]
            if w < 256:
                ipart[4 * b + g, :, w:256] = jnp.zeros((16, 256 - w), f32)
    irecv[me_d] = ipart[me_d]
    to_group(IN_RS, lambda p: ipart.at[p], irecv.at[me_d])

    magacc[...] = jnp.zeros_like(magacc)
    hg[...] = jnp.zeros_like(hg)
    CH = 256

    def rows_of(s):
        return pl.ds(pl.multiple_of(s * ROWS, ROWS), ROWS)

    def prepare(k):
        for h in range(2):
            for pair in range(2):
                if h == 0:
                    s0 = lax.rem(y + k + 3, LINE) * LINE + 2 * pair
                    s1 = s0 + 1
                else:
                    s0 = 2 * pair * LINE + lax.rem(x + k + 3, LINE)
                    s1 = s0 + LINE

                @pl.loop(0, QUART // CH)
                def _(c):
                    here = pl.ds(pl.multiple_of(c * CH, CH), CH)
                    c0 = cotb[h, s0, :, here].astype(f32)
                    c1 = cotb[h, s1, :, here].astype(f32)
                    for q in range(2):
                        a = c0[ROWS * q : ROWS * (q + 1)]
                        b = c1[ROWS * q : ROWS * (q + 1)]
                        at = pl.multiple_of(HALF * h + QUART * q + c * CH, CH)
                        cols = pl.ds(at, CH)
                        both = jnp.concatenate([a, b], axis=0) * scale_v[:, cols]
                        dst = pl.ds(pl.multiple_of(k * 96 + 48 * pair, 48), 48)
                        scaled[h, dst, pl.ds(pl.multiple_of(QUART * q + c * CH, CH), CH)] = both.astype(bf16)
                        m = a * prod[rows_of(s0), cols] + b * prod[rows_of(s1), cols]
                        magacc[:, cols] += jnp.sum(m.reshape(ROWS // 8, 8, CH), axis=0)

    def multiply(h, k0, n):
        for f in range(0, F, 256):
            w = min(256, F - f)
            r = dot(
                scaled[h, 96 * k0 : 96 * (k0 + n), :], w_v[f : f + w, HALF * h : HALF * (h + 1)], 1, 1
            )
            for k in range(k0, k0 + n):
                block = r[96 * (k - k0) : 96 * (k - k0 + 1)]
                if h == 0:
                    at = pl.multiple_of(lax.rem(y + k + 3, LINE) * 96, 96)
                    hg[pl.ds(at, 96), f : f + w] += block
                else:
                    for yy in range(LINE):
                        s = yy * LINE + lax.rem(x + k + 3, LINE)
                        hg[rows_of(s), f : f + w] += block[ROWS * yy : ROWS * (yy + 1)]

    for k in range(3):
        prepare(k)

    got(O_RS, orecv.at[fifteen])
    total = orecv[0]
    for t in range(1, GROUP):
        total = total + orecv[t]
    opl[me_t] = 2.0 * total
    to_plane(O_PL, lambda p: opl.at[me_t], opl.at[me_t])

    multiply(0, 0, 3)

    got(O_PL, opl.at[fifteen])
    ob[core, z] = opl[...].reshape(PEERS * 8, 128).astype(bf16)
    bundle = ob.at[core, z]

    @pl.loop(1, DEPTH)
    def _(d):
        pltpu.make_async_remote_copy(
            src_ref=bundle, dst_ref=bundle, send_sem=ph_send.at[O_Z], recv_sem=ph_recv.at[O_Z],
            device_id={"dp": lax.rem(z + d, DEPTH) * 2 + core}, device_id_type=MESH,
        ).start()

    got(IN_RS, irecv.at[fifteen])
    total = irecv[0]
    for t in range(1, GROUP):
        total = total + irecv[t]
    isum[...] = (2.0 * total).astype(bf16)
    iag[me_d] = isum[...]
    to_group(IN_AG, lambda p: isum, iag.at[me_d])

    multiply(1, 0, 3)

    for h in range(2):
        for j in range(4):
            last_across(h, j)
    prepare(3)
    magp[...] = jnp.sum(magacc[...], axis=0, keepdims=True)
    magr[me_t] = magp[:, my_cols(me_t)]
    to_plane(M_RS, lambda p: magp.at[:, my_cols(p)], magr.at[me_t])

    multiply(0, 3, 1)
    multiply(1, 3, 1)

    got(M_RS, magr.at[fifteen])
    total = magr[0]
    for t in range(1, PEERS):
        total = total + magr[t]
    magd[me_d] = total
    to_group(M_DP, lambda p: magd.at[me_d], magd.at[me_d])

    @pl.loop(0, TOK // 16)
    def _(i):
        rows = pl.ds(pl.multiple_of(i * 16, 16), 16)
        g = hg[rows, :]
        out_b[rows, :] = (g * u_v[rows, :]).astype(bf16)
        out_a[rows, :] = (g * v_v[rows, :]).astype(bf16)

    outs = [
        pltpu.make_async_copy(out_a, ggate_h, out_sem.at[0]),
        pltpu.make_async_copy(out_b, gup_h, out_sem.at[1]),
        pltpu.make_async_copy(gin_v, gin_h, out_sem.at[2]),
        pltpu.make_async_copy(gout_v, gout_h, out_sem.at[3]),
        pltpu.make_async_copy(gmag_v, gmag_h, out_sem.at[4]),
    ]
    outs[0].start()
    outs[1].start()

    got(O_Z, ob.at[0, pl.ds(0, DEPTH - 1)])
    other = pltpu.make_async_remote_copy(
        src_ref=ob.at[core], dst_ref=ob.at[core], send_sem=ph_send.at[O_CORE], recv_sem=ph_recv.at[O_CORE],
        device_id={"dp": z * 2 + 1 - core}, device_id_type=MESH,
    )
    other.start()

    got(M_DP, magd.at[fifteen])
    total = magd[0]
    for t in range(1, GROUP):
        total = total + magd[t]
    gmag_v[:, my_cols(me_t)] = total / norm_v[:, my_cols(me_t)]
    to_plane(M_AG, lambda p: gmag_v.at[:, my_cols(me_t)], gmag_v.at[:, my_cols(me_t)])

    got(IN_AG, iag.at[fifteen])
    for b in range(4):
        for g in range(4):
            w = 256 if g < 3 else 128
            gin_v[16 * b : 16 * b + 16, 256 * g : 256 * g + w] = iag[4 * b + g, :, 0:w].astype(f32)
    outs[2].start()

    other.wait_recv()
    for zz in range(DEPTH):
        for c in range(2):
            tile = ob[c, zz].astype(f32)
            for t in range(PEERS):
                at = COLS * t + 128 * c
                gout_v[8 * zz : 8 * zz + 8, at : at + 128] = tile[8 * t : 8 * t + 8]
    outs[3].start()

    got(M_AG, gmag_v.at[:, fifteen_cols])
    outs[4].start()

    for c in sent:
        c.wait_send()
    other.wait_send()
    left_here(J, jsend.at[fifteen])
    left_here(SQ_RS, sqp.at[:, fifteen_cols])
    left_here(SQ_AG, sqf.at[:, fifteen_cols])
    left_here(PR_RS, prs.at[fifteen])
    left_here(PR_AG, pra.at[fifteen])
    left_here(RC_AG, rca.at[fifteen])
    left_here(IN_RS, ipart.at[fifteen])
    left_here(IN_AG, iag.at[fifteen])
    left_here(O_RS, opart.at[fifteen])
    left_here(O_PL, opl.at[fifteen])
    left_here(O_Z, ob.at[0, pl.ds(0, DEPTH - 1)])
    left_here(M_RS, magp.at[:, fifteen_cols])
    left_here(M_DP, magd.at[fifteen])
    left_here(M_AG, gmag_v.at[:, fifteen_cols])
    for c in outs:
        c.wait()


def on_device(gate_act, up_act, cotangent, frozen_weight, adapter_in, adapter_out, magnitude):
    V = pltpu.VMEM
    scratch = [
        V((F, D), bf16), V((TOK, F), bf16), V((TOK, F), bf16), V((TOK, F), bf16),
        V((TOK, F), f32), V((TOK, F), f32), V((ROWS, D), bf16),
        V((2 * RANK, F), bf16), V((2 * RANK, D), bf16), V((1, D), f32), V((F, RANK), bf16),
        V((2, PEERS, 48, QUART), bf16), V((2, TOK, HALF), bf16), V((TOK, D), f32), V((TOK, F), f32),
        V((8, D), f32), V((8, D), f32), V((1, D), f32), V((1, D), f32),
        V((PEERS, 48, 128), bf16), V((PEERS, 48, 128), bf16), V((TOK, COLS), bf16),
        V((1, D), f32), V((PEERS, 1, COLS), f32), V((1, D), f32),
        V((PEERS, 16, 128), f32), V((PEERS, 16, 128), f32), V((PEERS, 16, 128), f32),
        V((16, 128), bf16), V((PEERS, 16, 128), bf16), V((TOK, 128), bf16),
        V((GROUP, 16, 256), f32), V((GROUP, 16, 256), f32), V((16, 256), bf16), V((GROUP, 16, 256), bf16),
        V((RANK, F), f32), V((GROUP, 8, 128), f32), V((GROUP, 8, 128), f32), V((PEERS, 8, 128), f32),
        V((2, DEPTH, 128, 128), bf16), V((RANK, D), f32),
        V((1, D), f32), V((PEERS, 1, COLS), f32), V((GROUP, 1, COLS), f32), V((1, D), f32),
        V((TOK, F), bf16), V((TOK, F), bf16),
        pltpu.SemaphoreType.DMA((8,)), pltpu.SemaphoreType.DMA((NWB,)), pltpu.SemaphoreType.DMA((5,)),
        pltpu.SemaphoreType.DMA((N_PHASES,)), pltpu.SemaphoreType.DMA((N_PHASES,)),
        pltpu.SemaphoreType.DMA((40,)), pltpu.SemaphoreType.DMA((40,)),
    ]
    hbm = pl.BlockSpec(memory_space=pl.ANY)
    outs = pl.pallas_call(
        kernel,
        out_shape=(
            jax.ShapeDtypeStruct((TOK, F), bf16),
            jax.ShapeDtypeStruct((TOK, F), bf16),
            jax.ShapeDtypeStruct((RANK, F), f32),
            jax.ShapeDtypeStruct((RANK, D), f32),
            jax.ShapeDtypeStruct((1, D), f32),
        ),
        in_specs=[hbm] * 7,
        out_specs=[hbm] * 5,
        scratch_shapes=scratch,
        compiler_params=pltpu.CompilerParams(
            collective_id=0, has_side_effects=True, vmem_limit_bytes=56 * 1024 * 1024
        ),
        cost_estimate=pl.CostEstimate(flops=7_000_000_000, bytes_accessed=14_000_000, transcendentals=400_000),
    )(gate_act, up_act, cotangent, frozen_weight, adapter_in, adapter_out, magnitude.reshape(1, D))
    return outs[0], outs[1], outs[2], outs[3], outs[4].reshape(D)


def solution(mesh):
    in_specs = (
        P("dp", "tensor"),
        P("dp", "tensor"),
        P(("dp", "tensor"), None),
        P("tensor", None),
        P(None, "tensor"),
        P(),
        P(),
    )
    out_specs = (P("dp", "tensor"), P("dp", "tensor"), P(None, "tensor"), P(), P())
    return jax.shard_map(
        on_device, mesh=mesh, in_specs=in_specs, out_specs=out_specs, check_vma=False
    )
```

time: 650 us -> 74.4 us (0.11)
  waiting for transfers between devices: 446 us -> 0 us
  blocking collectives: 138 us -> 0 us
  Pallas kernels: 0 us -> 64.3 us
  matrix products: 45.3 us -> 0 us
  between operations: 13.8 us -> 0.64 us
  local copies, waits for them, and re-layouts: 0.25 us -> 9.23 us
    psum x2 -> x0, waiting for transfers between devices: 359 us -> none  [the longest x1 258 us: on_device(): out_sum = lax.psum(out_part, ('dp', 'tensor'))]
    psum x2 -> x0, blocking collectives: 138 us -> none  [the longest x1 76.7 us: on_device(): magnitude_sum = lax.psum(magnitude_part, ('dp', 'tensor'))]
    unnamed x5 -> x0, waiting for transfers between devices: 87.5 us -> none
    pallas_call x0 -> x1, Pallas kernels: none -> 64.3 us  [on_device(): pl.pallas_call(kernel, out_shape=(jax.ShapeDtypeStruct((TOK, F), bf16), j...]
    dot_general x7 -> x0, matrix products: 45.3 us -> none  [the longest x6 32.6 us: contract(): lax.dot_general(left, right, (((left_dim,), (right_dim,)), ((), ())), pre...]
    unnamed x12 -> x5, local copies, waits for them, and re-layouts: 0.25 us -> 9.23 us
  transfers between devices with their start and end apart: 4 -> 0, of which waited for: 3 -> 0; matrix products, arithmetic and copies ran while one was open for 5% -> 0% of each run, Pallas kernels for 0% -> 0%
where the time goes in v1:
time: 74.4 us; the launch traced here: 74.2 us
  Pallas kernels  64.3 us (86%)
  local copies, waits for them, and re-layouts  9.23 us (12%)
    pallas_call x1, Pallas kernels, on_device(): pl.pallas_call(kernel, out_shape=(jax.ShapeDtypeStruct((TOK, F), bf16), j...  64.3 us
    unnamed x5, local copies, waits for them, and re-layouts  9.23 us

profile of v1, /device:TPU:1, one launch (start us, length us, event | category | flops | bytes accessed | tf_op | source)
XLA Modules:
  0.0 74.2 jit_solution(5130763674777850626)
XLA Ops:
  0.6 64.3 %shard_map.110 = (bf16[384,896]{1,0:T(8,128)(2,1)}, bf16[384,896]{1,0:T(8,128)(2,1)}, f32[64,896]{1,0:T(8,128)}, f32[64,4096]{1,0:T(8,128)}, f32[1,4096]{1,0:T(1,128)}) custom-call(bf16[384,896]{1,0:T(8,128)(2,1)} %gate_h.1, bf16[384,896]{1,0:T(8,128)(2,1)} %up_h.1, bf16[24,4096]{1,0:T(8,128)(2,1)} %cot_h.1, bf16[896,4096]{1,0:T(8,128)(2,1)} %w_h.1, ...), custom_call_target="tpu_custom_call" | custom-call | flops 7000000000 | bytes 14000000 | tf_op jit(solution)/shard_map/pallas_call | solution.py:522
  64.9 2.0 %copy.17 = bf16[384,896]{1,0:T(8,128)(2,1)} copy(bf16[384,896]{1,0:T(8,128)(2,1)} %get-tuple-element.20) | data formatting | bytes 1376256
  66.9 2.0 %copy.18 = bf16[384,896]{1,0:T(8,128)(2,1)} copy(bf16[384,896]{1,0:T(8,128)(2,1)} %get-tuple-element.21) | data formatting | bytes 1376256
  68.9 1.6 %copy.19 = f32[64,896]{1,0:T(8,128)} copy(f32[64,896]{1,0:T(8,128)} %get-tuple-element.22) | data formatting | bytes 458752
  70.6 2.3 %copy.20 = f32[64,4096]{1,0:T(8,128)} copy(f32[64,4096]{1,0:T(8,128)} %get-tuple-element.23) | data formatting | bytes 2097152
  72.8 1.3 %copy.21 = f32[4096]{0:T(1024)} copy(f32[4096]{0:T(1024)} %bitcast.2) | data formatting | bytes 32768

commit v2 on v1

v2 whole, which is shorter than its diff:
```python
import jax
import jax.numpy as jnp
from jax import lax
from jax.experimental import pallas as pl
from jax.experimental.pallas import tpu as pltpu
from jax.sharding import PartitionSpec as P

epsilon = 1e-06
MESH = pl.DeviceIdType.MESH
f32 = jnp.float32
bf16 = jnp.bfloat16

LINE = 4
PEERS = LINE * LINE
GROUP = 16
DEPTH = GROUP // 2
ROWS = 24
TOK = ROWS * PEERS
F = 896
D = 4096
RANK = 64
HALF = D // 2
QUART = D // 4
COLS = D // PEERS
WBLK = 128
NWB = F // WBLK

(J, SQ_RS, SQ_AG, PR_RS, PR_AG, RC_AG, IN_RS, IN_AG, O_RS, O_PL, O_Z, O_CORE, M_RS, M_DP, M_AG) = range(15)
N_PHASES = 15


def dot(a, b, da, db):
    return lax.dot_general(a, b, (((da,), (db,)), ((), ())), preferred_element_type=f32)


def kernel(
    gate_h, up_h, cot_h, w_h, ain_h, aout_h, mag_h,
    ggate_h, gup_h, gin_h, gout_h, gmag_h,
    w_v, gate_v, up_v, hid_v, u_v, v_v, cot_v, ain_v, aout_v, mag_v, aint_v,
    cotb, scaled, prod, hg, sqacc, magacc, scale_v, norm_v,
    jsend, jrecv, sjv, sqp, sqr, sqf, prs, prr, pra, rcs, rca, lv,
    ipart, irecv, isum, iag, gin_v, opart, orecv, oz, ob, gout_v,
    magp, magr, magd, gmag_v, out_a, out_b,
    loc_sem, w_sem, out_sem, ph_send, ph_recv, g_send, g_recv,
):
    me_t = lax.axis_index("tensor")
    me_d = lax.axis_index("dp")
    x = lax.rem(me_t, LINE)
    y = lax.div(me_t, LINE)
    z = lax.div(me_d, 2)
    core = lax.rem(me_d, 2)

    loads = [
        pltpu.make_async_copy(cot_h, cot_v, loc_sem.at[0]),
        pltpu.make_async_copy(ain_h, ain_v.at[pl.ds(0, RANK)], loc_sem.at[1]),
        pltpu.make_async_copy(aout_h, aout_v.at[pl.ds(0, RANK)], loc_sem.at[2]),
        pltpu.make_async_copy(gate_h, gate_v, loc_sem.at[3]),
        pltpu.make_async_copy(up_h, up_v, loc_sem.at[4]),
        pltpu.make_async_copy(ain_h, ain_v.at[pl.ds(RANK, RANK)], loc_sem.at[5]),
        pltpu.make_async_copy(aout_h, aout_v.at[pl.ds(RANK, RANK)], loc_sem.at[6]),
        pltpu.make_async_copy(mag_h, mag_v, loc_sem.at[7]),
    ]

    def w_copy(i):
        rows = pl.ds(pl.multiple_of(i * WBLK, WBLK), WBLK)
        return pltpu.make_async_copy(w_h.at[rows], w_v.at[rows], w_sem.at[i])

    for c in loads[0:3]:
        c.start()
    for i in range(NWB):
        w_copy(i).start()
    for c in loads[3:]:
        c.start()

    barrier = pltpu.get_barrier_semaphore()

    @pl.loop(1, PEERS)
    def _(d):
        pl.semaphore_signal(barrier, inc=1, device_id={"tensor": lax.rem(me_t + d, PEERS)}, device_id_type=MESH)

    @pl.loop(1, GROUP)
    def _(d):
        pl.semaphore_signal(barrier, inc=1, device_id={"dp": lax.rem(me_d + d, GROUP)}, device_id_type=MESH)

    loads[0].wait()
    for h in range(2):
        left = cot_v[:, HALF * h : HALF * h + QUART].astype(f32)
        right = cot_v[:, HALF * h + QUART : HALF * (h + 1)].astype(f32)
        cotb[h, me_t] = jnp.concatenate([left, right], axis=0).astype(bf16)

    def slot(h, along, across):
        if h == 0:
            return lax.rem(y + across + LINE, LINE) * LINE + lax.rem(x + along + LINE, LINE)
        return lax.rem(y + along + LINE, LINE) * LINE + lax.rem(x + across + LINE, LINE)

    def move(h, along, across, part, to, sem):
        if part is None:
            ref = cotb.at[h, slot(h, along, across)]
        else:
            ref = cotb.at[h, slot(h, along, across), :, pl.ds(part * (QUART // 2), QUART // 2)]
        return pltpu.make_async_remote_copy(
            src_ref=ref, dst_ref=ref, send_sem=g_send.at[20 * h + sem], recv_sem=g_recv.at[20 * h + sem],
            device_id={"tensor": to}, device_id_type=MESH,
        )

    sent = []

    def go(h, along, across, part, to, sem):
        c = move(h, along, across, part, to, sem)
        c.start()
        sent.append(c)

    def arrive(h, along, across, part, sem):
        move(h, along, across, part, slot(h, 0, 1), sem).wait_recv()

    offsets = (0, -1, 1, 2)

    def send_across(h, j):
        go(h, offsets[j], 0, None, slot(h, 0, 1), 4 + 4 * j)
        go(h, offsets[j], 0, None, slot(h, 0, -1), 5 + 4 * j)

    def forward_across(h, j):
        arrive(h, offsets[j], -1, None, 4 + 4 * j)
        go(h, offsets[j], -1, 0, slot(h, 0, 1), 6 + 4 * j)
        arrive(h, offsets[j], 1, None, 5 + 4 * j)
        go(h, offsets[j], 1, 1, slot(h, 0, -1), 7 + 4 * j)

    def last_across(h, j):
        arrive(h, offsets[j], 2, 0, 6 + 4 * j)
        arrive(h, offsets[j], 2, 1, 7 + 4 * j)

    def exchange(phase, axis, src, dst, me, n):
        def one(p):
            return pltpu.make_async_remote_copy(
                src_ref=src(p), dst_ref=dst, send_sem=ph_send.at[phase], recv_sem=ph_recv.at[phase],
                device_id={axis: p}, device_id_type=MESH,
            )

        @pl.loop(1, n)
        def _(d):
            one(lax.rem(me + d, n)).start()

    def got(phase, ref):
        pltpu.make_async_copy(ref, ref, ph_recv.at[phase]).wait()

    def left_here(phase, ref):
        pltpu.make_async_copy(ref, ref, ph_send.at[phase]).wait()

    def to_plane(phase, src, dst):
        exchange(phase, "tensor", src, dst, me_t, PEERS)

    def to_group(phase, src, dst):
        exchange(phase, "dp", src, dst, me_d, GROUP)

    def my_cols(p):
        return pl.ds(pl.multiple_of(p * COLS, COLS), COLS)

    fifteen = pl.ds(0, 15)
    fifteen_cols = pl.ds(0, 15 * COLS)

    def sum_of(ref, n):
        total = ref[0]
        for t in range(1, n):
            total = total + ref[t]
        return total

    low_lanes = lax.broadcasted_iota(jnp.int32, (8, 128), 1) < RANK

    def gate_and_up():
        loads[3].wait()
        loads[4].wait()

        @pl.loop(0, TOK // 16)
        def _(i):
            rows = pl.ds(pl.multiple_of(i * 16, 16), 16)
            g = gate_v[rows, :].astype(f32)
            u = up_v[rows, :].astype(f32)
            s = 1.0 / (1.0 + jnp.exp(-g))
            gs = g * s
            hid_v[rows, :] = (gs * u).astype(bf16)
            u_v[rows, :] = gs
            v_v[rows, :] = u * s * (1.0 + g * (1.0 - s))

    def project():
        loads[5].wait()
        part = dot(hid_v[...], ain_v[...], 1, 1)
        for t in range(PEERS):
            r = ROWS * t
            prs[t, 0:8] = jnp.where(low_lanes, part[r : r + 8], part[r + 8 : r + 16])
            prs[t, 8:16] = part[r + 16 : r + 24]
        prr[me_t] = prs[me_t]
        to_plane(PR_RS, lambda p: prs.at[p], prr.at[me_t])

    def start_adjust():
        loads[1].wait()
        aint_v[...] = (2.0 * jnp.transpose(ain_v[0:RANK, :].astype(f32), (1, 0))).astype(bf16)
        sqacc[...] = jnp.zeros_like(sqacc)
        loads[2].wait()

    def adjust(i):
        w_copy(i).wait()
        rows = pl.ds(pl.multiple_of(i * WBLK, WBLK), WBLK)
        lhs = aint_v[rows, :]
        for c in range(8):
            cols = slice(512 * c, 512 * (c + 1))
            a = w_v[rows, cols].astype(f32) + dot(lhs, aout_v[0:RANK, cols], 1, 0)
            w_v[rows, cols] = a.astype(bf16)
            sqacc[:, cols] += jnp.sum((a * a).reshape(WBLK // 8, 8, 512), axis=0)

    def send_squares():
        sqp[...] = jnp.sum(sqacc[...], axis=0, keepdims=True)
        sqr[me_t] = sqp[:, my_cols(me_t)]
        to_plane(SQ_RS, lambda p: sqp.at[:, my_cols(p)], sqr.at[me_t])

    def sum_squares():
        got(SQ_RS, sqr.at[fifteen])
        sqf[:, my_cols(me_t)] = sum_of(sqr, PEERS)
        to_plane(SQ_AG, lambda p: sqf.at[:, my_cols(me_t)], sqf.at[:, my_cols(me_t)])

    def send_columns():
        for t in range(PEERS):
            left = cot_v[:, COLS * t : COLS * t + 128].astype(f32)
            right = cot_v[:, COLS * t + 128 : COLS * (t + 1)].astype(f32)
            jsend[t] = jnp.concatenate([left, right], axis=0).astype(bf16)
        jrecv[me_t] = jsend[me_t]
        to_plane(J, lambda p: jsend.at[p], jrecv.at[me_t])

    def first_along():
        for h in range(2):
            arrive(h, -1, 0, None, 0)
            go(h, -1, 0, 0, slot(h, 1, 0), 2)
            arrive(h, 1, 0, None, 1)
            go(h, 1, 0, 1, slot(h, -1, 0), 3)
        for h in range(2):
            send_across(h, 1)
            send_across(h, 2)

    def last_along():
        for h in range(2):
            arrive(h, 2, 0, 0, 2)
            arrive(h, 2, 0, 1, 3)
            send_across(h, 3)

    def sum_projected():
        got(PR_RS, prr.at[fifteen])
        pra[me_t] = sum_of(prr, PEERS)
        to_plane(PR_AG, lambda p: pra.at[me_t], pra.at[me_t])

    def produce(i):
        cols = pl.ds(pl.multiple_of(i * 256, 256), 256)
        prod[:, cols] = dot(hid_v[...], w_v[:, cols], 1, 0)

    def out_grad():
        got(J, jrecv.at[fifteen])
        got(PR_AG, pra.at[fifteen])
        for t in range(0, PEERS, 2):
            c0 = jrecv[t].astype(f32)
            c1 = jrecv[t + 1].astype(f32)
            sjv[ROWS * t : ROWS * (t + 2), 0:128] = jnp.concatenate([c0[0:24], c1[0:24]], axis=0).astype(bf16)
            sjv[ROWS * t : ROWS * (t + 2), 128:256] = jnp.concatenate([c0[24:48], c1[24:48]], axis=0).astype(bf16)

            def both(tile, last):
                turned = pltpu.roll(tile, RANK, 1)
                return [jnp.where(low_lanes, tile, turned), jnp.where(low_lanes, turned, tile), last]

            rows = jnp.concatenate(
                both(pra[t, 0:8], pra[t, 8:16]) + both(pra[t + 1, 0:8], pra[t + 1, 8:16]), axis=0
            )
            high = rows.astype(bf16).astype(f32)
            lanes = lax.broadcasted_iota(jnp.int32, rows.shape, 1) < RANK
            lv[ROWS * t : ROWS * (t + 2), :] = jnp.where(lanes, high, rows - high).astype(bf16)
        o = dot(lv[...], sjv[...], 0, 0)
        o = o[0:RANK] + o[RANK:]
        for p in range(GROUP):
            opart[p] = o[8 * (p // 2) : 8 * (p // 2) + 8, 128 * (p % 2) : 128 * (p % 2) + 128]
        orecv[me_d] = opart[me_d]
        to_group(O_RS, lambda p: opart.at[p], orecv.at[me_d])

    def sum_out_grad():
        got(O_RS, orecv.at[fifteen])
        mine = pl.ds(pl.multiple_of(me_t * COLS + core * 128, 128), 128)
        oz[z] = 2.0 * sum_of(orecv, GROUP) * scale_v[:, mine]

        @pl.loop(1, DEPTH)
        def _(d):
            pltpu.make_async_remote_copy(
                src_ref=oz.at[z], dst_ref=oz.at[z], send_sem=ph_send.at[O_Z], recv_sem=ph_recv.at[O_Z],
                device_id={"dp": lax.rem(z + d, DEPTH) * 2 + core}, device_id_type=MESH,
            ).start()

    def spread_out_grad():
        got(O_Z, oz.at[pl.ds(0, DEPTH - 1)])
        ob[core, me_t] = oz[...].reshape(RANK, 128).astype(bf16)
        to_plane(O_PL, lambda p: ob.at[core, me_t], ob.at[core, me_t])

    other = pltpu.make_async_remote_copy(
        src_ref=ob.at[core], dst_ref=ob.at[core], send_sem=ph_send.at[O_CORE], recv_sem=ph_recv.at[O_CORE],
        device_id={"dp": z * 2 + 1 - core}, device_id_type=MESH,
    )

    def swap_out_grad():
        got(O_PL, ob.at[0, fifteen])
        other.start()

    def column_scale():
        loads[7].wait()
        got(SQ_AG, sqf.at[:, fifteen_cols])
        norm_v[...] = jnp.sqrt(sqf[...] + epsilon)
        scale_v[...] = mag_v[...] / norm_v[...]

    def send_rank():
        loads[6].wait()
        rank = jnp.zeros((32, 128), f32)
        for c in range(8):
            cols = slice(512 * c, 512 * (c + 1))
            s = cot_v[:, cols].astype(f32) * scale_v[:, cols]
            s = jnp.concatenate([s, jnp.zeros((8, 512), f32)], axis=0).astype(bf16)
            rank = rank + dot(s, aout_v[:, cols], 1, 1)
        rcs[...] = jnp.concatenate([jnp.where(low_lanes, rank[0:8], rank[8:16]), rank[16:24]], axis=0).astype(bf16)
        rca[me_t] = rcs[...]
        to_plane(RC_AG, lambda p: rcs, rca.at[me_t])

    def in_grad():
        got(RC_AG, rca.at[fifteen])
        for t in range(0, PEERS, 2):
            c0 = rca[t].astype(f32)
            c1 = rca[t + 1].astype(f32)
            rows = jnp.concatenate(
                [c0[0:8], pltpu.roll(c0[0:8], RANK, 1), c0[8:16], c1[0:8], pltpu.roll(c1[0:8], RANK, 1), c1[8:16]], axis=0
            )
            lv[ROWS * t : ROWS * (t + 2), :] = rows.astype(bf16)
        for g in range(4):
            w = 256 if g < 3 else 128
            o = dot(lv[...], hid_v[:, 256 * g : 256 * g + w], 0, 0).astype(bf16)
            for b in range(4):
                ipart[4 * b + g, :, 0:w] = o[16 * b : 16 * b + 16]
                if w < 256:
                    ipart[4 * b + g, :, w:256] = jnp.zeros((16, 256 - w), bf16)
        irecv[me_d] = ipart[me_d]
        to_group(IN_RS, lambda p: ipart.at[p], irecv.at[me_d])

    def sum_in_grad():
        got(IN_RS, irecv.at[fifteen])
        total = irecv[0].astype(f32)
        for t in range(1, GROUP):
            total = total + irecv[t].astype(f32)
        isum[...] = (2.0 * total).astype(bf16)
        iag[me_d] = isum[...]
        to_group(IN_AG, lambda p: isum, iag.at[me_d])

    CH = 256

    def rows_of(s):
        return pl.ds(pl.multiple_of(s * ROWS, ROWS), ROWS)

    def prepare(k):
        for h in range(2):
            for pair in range(2):
                if h == 0:
                    s0 = lax.rem(y + k + 3, LINE) * LINE + 2 * pair
                    s1 = s0 + 1
                else:
                    s0 = 2 * pair * LINE + lax.rem(x + k + 3, LINE)
                    s1 = s0 + LINE

                @pl.loop(0, QUART // CH)
                def _(c):
                    here = pl.ds(pl.multiple_of(c * CH, CH), CH)
                    c0 = cotb[h, s0, :, here].astype(f32)
                    c1 = cotb[h, s1, :, here].astype(f32)
                    for q in range(2):
                        a = c0[ROWS * q : ROWS * (q + 1)]
                        b = c1[ROWS * q : ROWS * (q + 1)]
                        at = pl.multiple_of(HALF * h + QUART * q + c * CH, CH)
                        cols = pl.ds(at, CH)
                        both = jnp.concatenate([a, b], axis=0) * scale_v[:, cols]
                        dst = pl.ds(pl.multiple_of(k * 96 + 48 * pair, 48), 48)
                        scaled[h, dst, pl.ds(pl.multiple_of(QUART * q + c * CH, CH), CH)] = both.astype(bf16)
                        m = a * prod[rows_of(s0), cols] + b * prod[rows_of(s1), cols]
                        magacc[:, cols] += jnp.sum(m.reshape(ROWS // 8, 8, CH), axis=0)

    def multiply(h, first=0, last=F):
        for f in range(first, last, 256):
            w = min(256, F - f)
            r = dot(scaled[h], w_v[f : f + w, HALF * h : HALF * (h + 1)], 1, 1)
            for k in range(LINE):
                block = r[96 * k : 96 * (k + 1)]
                if h == 0:
                    at = pl.multiple_of(lax.rem(y + k + 3, LINE) * 96, 96)
                    hg[pl.ds(at, 96), f : f + w] = block
                else:
                    for yy in range(LINE):
                        s = yy * LINE + lax.rem(x + k + 3, LINE)
                        hg[rows_of(s), f : f + w] += block[ROWS * yy : ROWS * (yy + 1)]

    def send_mag():
        magp[...] = jnp.sum(magacc[...], axis=0, keepdims=True)
        magr[me_t] = magp[:, my_cols(me_t)]
        to_plane(M_RS, lambda p: magp.at[:, my_cols(p)], magr.at[me_t])

    def sum_mag_plane():
        got(M_RS, magr.at[fifteen])
        magd[me_d] = sum_of(magr, PEERS)
        to_group(M_DP, lambda p: magd.at[me_d], magd.at[me_d])

    def sum_mag_group():
        got(M_DP, magd.at[fifteen])
        gmag_v[:, my_cols(me_t)] = sum_of(magd, GROUP) / norm_v[:, my_cols(me_t)]
        to_plane(M_AG, lambda p: gmag_v.at[:, my_cols(me_t)], gmag_v.at[:, my_cols(me_t)])

    outs = [
        pltpu.make_async_copy(out_a, ggate_h, out_sem.at[0]),
        pltpu.make_async_copy(out_b, gup_h, out_sem.at[1]),
        pltpu.make_async_copy(gin_v, gin_h, out_sem.at[2]),
        pltpu.make_async_copy(gout_v, gout_h, out_sem.at[3]),
        pltpu.make_async_copy(gmag_v, gmag_h, out_sem.at[4]),
    ]

    def large_grads():
        @pl.loop(0, TOK // 16)
        def _(i):
            rows = pl.ds(pl.multiple_of(i * 16, 16), 16)
            g = hg[rows, :]
            out_b[rows, :] = (g * u_v[rows, :]).astype(bf16)
            out_a[rows, :] = (g * v_v[rows, :]).astype(bf16)

        outs[0].start()
        outs[1].start()

    def finish_in_grad():
        got(IN_AG, iag.at[fifteen])
        for b in range(4):
            for g in range(4):
                w = 256 if g < 3 else 128
                gin_v[16 * b : 16 * b + 16, 256 * g : 256 * g + w] = iag[4 * b + g, :, 0:w].astype(f32)
        outs[2].start()

    def finish_out_grad():
        other.wait_recv()
        for t in range(PEERS):
            for c in range(2):
                at = COLS * t + 128 * c
                gout_v[:, at : at + 128] = ob[c, t].astype(f32)
        outs[3].start()

    def finish_mag():
        got(M_AG, gmag_v.at[:, fifteen_cols])
        outs[4].start()

    start_adjust()
    adjust(0)

    pl.semaphore_wait(barrier, PEERS + GROUP - 2)
    for h in range(2):
        go(h, 0, 0, None, slot(h, 1, 0), 0)
        go(h, 0, 0, None, slot(h, -1, 0), 1)
    pl.loop(1, 5)(adjust)
    for h in range(2):
        send_across(h, 0)
    pl.loop(5, NWB)(adjust)
    send_squares()
    gate_and_up()
    project()
    pl.loop(0, 5)(produce)
    first_along()
    send_columns()
    pl.loop(5, 8)(produce)
    sum_squares()
    for h in range(2):
        forward_across(h, 0)
    sum_projected()
    last_along()
    pl.loop(8, 16)(produce)
    for h in range(2):
        forward_across(h, 1)
        forward_across(h, 2)
    column_scale()
    send_rank()
    out_grad()
    magacc[...] = jnp.zeros_like(magacc)
    prepare(1)
    for h in range(2):
        forward_across(h, 3)
    prepare(0)
    prepare(2)
    in_grad()
    for h in range(2):
        for j in range(4):
            last_across(h, j)
    prepare(3)
    send_mag()
    sum_out_grad()
    multiply(0)
    sum_mag_plane()
    spread_out_grad()
    sum_in_grad()
    multiply(1)
    large_grads()
    sum_mag_group()
    swap_out_grad()
    finish_in_grad()
    finish_out_grad()
    finish_mag()

    for c in sent:
        c.wait_send()
    other.wait_send()
    left_here(J, jsend.at[fifteen])
    left_here(SQ_RS, sqp.at[:, fifteen_cols])
    left_here(SQ_AG, sqf.at[:, fifteen_cols])
    left_here(PR_RS, prs.at[fifteen])
    left_here(PR_AG, pra.at[fifteen])
    left_here(RC_AG, rca.at[fifteen])
    left_here(IN_RS, ipart.at[fifteen])
    left_here(IN_AG, iag.at[fifteen])
    left_here(O_RS, opart.at[fifteen])
    left_here(O_PL, ob.at[0, fifteen])
    left_here(O_Z, oz.at[pl.ds(0, DEPTH - 1)])
    left_here(M_RS, magp.at[:, fifteen_cols])
    left_here(M_DP, magd.at[fifteen])
    left_here(M_AG, gmag_v.at[:, fifteen_cols])
    for c in outs:
        c.wait()


def hand_over(*refs):
    src, dst, held, sem_in, sem_out = refs[0:5], refs[5:10], refs[10:15], refs[15], refs[16]
    into = [pltpu.make_async_copy(src[i], held[i], sem_in.at[i]) for i in range(5)]
    out = [pltpu.make_async_copy(held[i], dst[i], sem_out.at[i]) for i in range(5)]
    for c in into:
        c.start()
    for i in range(5):
        into[i].wait()
        out[i].start()
    for c in out:
        c.wait()


def on_device(gate_act, up_act, cotangent, frozen_weight, adapter_in, adapter_out, magnitude):
    V = pltpu.VMEM
    scratch = [
        V((F, D), bf16), V((TOK, F), bf16), V((TOK, F), bf16), V((TOK, F), bf16),
        V((TOK, F), f32), V((TOK, F), f32), V((ROWS, D), bf16),
        V((2 * RANK, F), bf16), V((2 * RANK, D), bf16), V((1, D), f32), V((F, RANK), bf16),
        V((2, PEERS, 48, QUART), bf16), V((2, TOK, HALF), bf16), V((TOK, D), f32), V((TOK, F), f32),
        V((8, D), f32), V((8, D), f32), V((1, D), f32), V((1, D), f32),
        V((PEERS, 48, 128), bf16), V((PEERS, 48, 128), bf16), V((TOK, COLS), bf16),
        V((1, D), f32), V((PEERS, 1, COLS), f32), V((1, D), f32),
        V((PEERS, 16, 128), f32), V((PEERS, 16, 128), f32), V((PEERS, 16, 128), f32),
        V((16, 128), bf16), V((PEERS, 16, 128), bf16), V((TOK, 128), bf16),
        V((GROUP, 16, 256), bf16), V((GROUP, 16, 256), bf16), V((16, 256), bf16), V((GROUP, 16, 256), bf16),
        V((RANK, F), f32), V((GROUP, 8, 128), f32), V((GROUP, 8, 128), f32), V((DEPTH, 8, 128), f32),
        V((2, PEERS, RANK, 128), bf16), V((RANK, D), f32),
        V((1, D), f32), V((PEERS, 1, COLS), f32), V((GROUP, 1, COLS), f32), V((1, D), f32),
        V((TOK, F), bf16), V((TOK, F), bf16),
        pltpu.SemaphoreType.DMA((8,)), pltpu.SemaphoreType.DMA((NWB,)), pltpu.SemaphoreType.DMA((5,)),
        pltpu.SemaphoreType.DMA((N_PHASES,)), pltpu.SemaphoreType.DMA((N_PHASES,)),
        pltpu.SemaphoreType.DMA((40,)), pltpu.SemaphoreType.DMA((40,)),
    ]
    hbm = pl.BlockSpec(memory_space=pl.ANY)
    outs = pl.pallas_call(
        kernel,
        out_shape=(
            jax.ShapeDtypeStruct((TOK, F), bf16),
            jax.ShapeDtypeStruct((TOK, F), bf16),
            jax.ShapeDtypeStruct((RANK, F), f32),
            jax.ShapeDtypeStruct((RANK, D), f32),
            jax.ShapeDtypeStruct((1, D), f32),
        ),
        in_specs=[hbm] * 7,
        out_specs=[hbm] * 5,
        scratch_shapes=scratch,
        compiler_params=pltpu.CompilerParams(
            collective_id=0, has_side_effects=True, vmem_limit_bytes=60 * 1024 * 1024
        ),
        cost_estimate=pl.CostEstimate(flops=7_000_000_000, bytes_accessed=14_000_000, transcendentals=400_000),
    )(gate_act, up_act, cotangent, frozen_weight, adapter_in, adapter_out, magnitude.reshape(1, D))
    outs = pl.pallas_call(
        hand_over,
        out_shape=[jax.ShapeDtypeStruct(o.shape, o.dtype) for o in outs],
        in_specs=[hbm] * 5,
        out_specs=[hbm] * 5,
        scratch_shapes=[V(o.shape, o.dtype) for o in outs]
        + [pltpu.SemaphoreType.DMA((5,)), pltpu.SemaphoreType.DMA((5,))],
        compiler_params=pltpu.CompilerParams(vmem_limit_bytes=60 * 1024 * 1024),
    )(*outs)
    return outs[0], outs[1], outs[2], outs[3], outs[4].reshape(D)


def solution(mesh):
    in_specs = (
        P("dp", "tensor"),
        P("dp", "tensor"),
        P(("dp", "tensor"), None),
        P("tensor", None),
        P(None, "tensor"),
        P(),
        P(),
    )
    out_specs = (P("dp", "tensor"), P("dp", "tensor"), P(None, "tensor"), P(), P())
    return jax.shard_map(
        on_device, mesh=mesh, in_specs=in_specs, out_specs=out_specs, check_vma=False
    )
```

time: 74.4 us -> 55.4 us (0.74)
  Pallas kernels: 64.3 us -> 54.7 us
  local copies, waits for them, and re-layouts: 9.23 us -> 0 us
    pallas_call x1, Pallas kernels: 64.3 us -> 51.9 us  [on_device(): pl.pallas_call(kernel, out_shape=(jax.ShapeDtypeStruct((TOK, F), bf16), j...]
    unnamed x5 -> x0, local copies, waits for them, and re-layouts: 9.23 us -> none
    pallas_call x0 -> x1, Pallas kernels: none -> 2.77 us  [on_device(): pl.pallas_call(hand_over, out_shape=[jax.ShapeDtypeStruct(o.shape, o.dtyp...]
where the time goes in v2:
time: 55.4 us; the launch traced here: 55.3 us
  Pallas kernels  54.7 us (99%)
  between operations  0.64 us (1%)
    pallas_call x1, Pallas kernels, on_device(): pl.pallas_call(kernel, out_shape=(jax.ShapeDtypeStruct((TOK, F), bf16), j...  51.9 us
    pallas_call x1, Pallas kernels, on_device(): pl.pallas_call(hand_over, out_shape=[jax.ShapeDtypeStruct(o.shape, o.dtyp...  2.77 us

profile of v2, /device:TPU:1, one launch (start us, length us, event | category | flops | bytes accessed | tf_op | source)
XLA Modules:
  0.0 55.3 jit_solution(9977870296815497921)
XLA Ops:
  0.6 51.9 %shard_map.110 = (bf16[384,896]{1,0:T(8,128)(2,1)}, bf16[384,896]{1,0:T(8,128)(2,1)}, f32[64,896]{1,0:T(8,128)}, f32[64,4096]{1,0:T(8,128)}, f32[1,4096]{1,0:T(1,128)}) custom-call(bf16[384,896]{1,0:T(8,128)(2,1)} %gate_h.1, bf16[384,896]{1,0:T(8,128)(2,1)} %up_h.1, bf16[24,4096]{1,0:T(8,128)(2,1)} %cot_h.1, bf16[896,4096]{1,0:T(8,128)(2,1)} %w_h.1, ...), custom_call_target="tpu_custom_call" | custom-call | flops 7000000000 | bytes 14000000 | tf_op jit(solution)/shard_map/pallas_call | solution.py:561
  52.5 2.8 %shard_map.111 = (bf16[384,896]{1,0:T(8,128)(2,1)}, bf16[384,896]{1,0:T(8,128)(2,1)}, f32[64,896]{1,0:T(8,128)}, f32[64,4096]{1,0:T(8,128)}, f32[1,4096]{1,0:T(1,128)}) custom-call(bf16[384,896]{1,0:T(8,128)(2,1)} %get-tuple-element.15.refs_0_, bf16[384,896]{1,0:T(8,128)(2,1)} %get-tuple-element.16.refs_1_, f32[64,896]{1,0:T(8,128)} %get-tuple-element.17.refs_2_, ...), custom_call_target="tpu_custom_call" | custom-call | tf_op jit(solution)/shard_map/pallas_call | solution.py:578

commit v3 on v2

--- a/solution.py
+++ b/solution.py
@@ -37,8 +37,8 @@
     gate_h, up_h, cot_h, w_h, ain_h, aout_h, mag_h,
     ggate_h, gup_h, gin_h, gout_h, gmag_h,
     w_v, gate_v, up_v, hid_v, u_v, v_v, cot_v, ain_v, aout_v, mag_v, aint_v,
-    cotb, scaled, prod, hg, sqacc, magacc, scale_v, norm_v,
-    jsend, jrecv, sjv, sqp, sqr, sqf, prs, prr, pra, rcs, rca, lv,
+    cotb, scaled, prod, hg, magacc, scale_v, norm_v,
+    jsend, jrecv, wj_v, sqr, sqf, prs, prr, pra, rcs, rca, lv,
     ipart, irecv, isum, iag, gin_v, opart, orecv, oz, ob, gout_v,
     magp, magr, magd, gmag_v, out_a, out_b,
     loc_sem, w_sem, out_sem, ph_send, ph_recv, g_send, g_recv,
@@ -65,11 +65,16 @@
         rows = pl.ds(pl.multiple_of(i * WBLK, WBLK), WBLK)
         return pltpu.make_async_copy(w_h.at[rows], w_v.at[rows], w_sem.at[i])
 
+    my_part = pl.ds(pl.multiple_of(me_d * COLS, COLS), COLS)
+    wj_copy = pltpu.make_async_copy(w_h.at[:, my_part], wj_v, loc_sem.at[8])
     for c in loads[0:3]:
+        c.start()
+    wj_copy.start()
+    for c in loads[3:6]:
         c.start()
     for i in range(NWB):
         w_copy(i).start()
-    for c in loads[3:]:
+    for c in loads[6:]:
         c.start()
 
     barrier = pltpu.get_barrier_semaphore()
@@ -191,11 +196,25 @@
         prr[me_t] = prs[me_t]
         to_plane(PR_RS, lambda p: prs.at[p], prr.at[me_t])
 
-    def start_adjust():
+    def square_part():
         loads[1].wait()
         aint_v[...] = (2.0 * jnp.transpose(ain_v[0:RANK, :].astype(f32), (1, 0))).astype(bf16)
-        sqacc[...] = jnp.zeros_like(sqacc)
         loads[2].wait()
+        wj_copy.wait()
+        squares = jnp.zeros((8, COLS), f32)
+        for i in range(NWB):
+            rows = slice(WBLK * i, WBLK * (i + 1))
+            a = wj_v[rows, :].astype(f32) + dot(aint_v[rows, :], aout_v[0:RANK, my_part], 1, 0)
+            squares = squares + jnp.sum((a * a).reshape(WBLK // 8, 8, COLS), axis=0)
+        sqr[me_t] = jnp.sum(squares, axis=0, keepdims=True)
+
+    def send_squares():
+        to_plane(SQ_RS, lambda p: sqr.at[me_t], sqr.at[me_t])
+
+    def sum_squares():
+        got(SQ_RS, sqr.at[fifteen])
+        sqf[:, my_part] = sum_of(sqr, PEERS)
+        to_group(SQ_AG, lambda p: sqf.at[:, my_part], sqf.at[:, my_part])
 
     def adjust(i):
         w_copy(i).wait()
@@ -205,25 +224,26 @@
             cols = slice(512 * c, 512 * (c + 1))
             a = w_v[rows, cols].astype(f32) + dot(lhs, aout_v[0:RANK, cols], 1, 0)
             w_v[rows, cols] = a.astype(bf16)
-            sqacc[:, cols] += jnp.sum((a * a).reshape(WBLK // 8, 8, 512), axis=0)
-
-    def send_squares():
-        sqp[...] = jnp.sum(sqacc[...], axis=0, keepdims=True)
-        sqr[me_t] = sqp[:, my_cols(me_t)]
-        to_plane(SQ_RS, lambda p: sqp.at[:, my_cols(p)], sqr.at[me_t])
-
-    def sum_squares():
-        got(SQ_RS, sqr.at[fifteen])
-        sqf[:, my_cols(me_t)] = sum_of(sqr, PEERS)
-        to_plane(SQ_AG, lambda p: sqf.at[:, my_cols(me_t)], sqf.at[:, my_cols(me_t)])
 
     def send_columns():
-        for t in range(PEERS):
-            left = cot_v[:, COLS * t : COLS * t + 128].astype(f32)
-            right = cot_v[:, COLS * t + 128 : COLS * (t + 1)].astype(f32)
-            jsend[t] = jnp.concatenate([left, right], axis=0).astype(bf16)
-        jrecv[me_t] = jsend[me_t]
-        to_plane(J, lambda p: jsend.at[p], jrecv.at[me_t])
+        for h in range(2):
+            for d in range(LINE):
+                to = slot(h, 0, d)
+                low = to < PEERS // 2
+                at = pl.ds(pl.multiple_of(lax.rem(to, PEERS // 2) * 128, 128), 128)
+                rows = []
+                for m in range(LINE):
+                    c = cotb[h, y * LINE + m if h == 0 else m * LINE + x, :, at].astype(f32)
+                    rows.append(jnp.where(low, c[0:ROWS], c[ROWS : 2 * ROWS]))
+                jsend[h, d] = jnp.concatenate(rows, axis=0).astype(bf16)
+        for h in range(2):
+            me = y if h == 0 else x
+            jrecv[h, me] = jsend[h, 0]
+            for d in range(1, LINE):
+                pltpu.make_async_remote_copy(
+                    src_ref=jsend.at[h, d], dst_ref=jrecv.at[h, me], send_sem=ph_send.at[J], recv_sem=ph_recv.at[J],
+                    device_id={"tensor": slot(h, 0, d)}, device_id_type=MESH,
+                ).start()
 
     def first_along():
         for h in range(2):
@@ -231,15 +251,11 @@
             go(h, -1, 0, 0, slot(h, 1, 0), 2)
             arrive(h, 1, 0, None, 1)
             go(h, 1, 0, 1, slot(h, -1, 0), 3)
-        for h in range(2):
-            send_across(h, 1)
-            send_across(h, 2)
 
     def last_along():
         for h in range(2):
             arrive(h, 2, 0, 0, 2)
             arrive(h, 2, 0, 1, 3)
-            send_across(h, 3)
 
     def sum_projected():
         got(PR_RS, prr.at[fifteen])
@@ -251,34 +267,32 @@
         prod[:, cols] = dot(hid_v[...], w_v[:, cols], 1, 0)
 
     def out_grad():
-        got(J, jrecv.at[fifteen])
+        got(J, jrecv.at[:, pl.ds(0, LINE - 1)])
         got(PR_AG, pra.at[fifteen])
-        for t in range(0, PEERS, 2):
-            c0 = jrecv[t].astype(f32)
-            c1 = jrecv[t + 1].astype(f32)
-            sjv[ROWS * t : ROWS * (t + 2), 0:128] = jnp.concatenate([c0[0:24], c1[0:24]], axis=0).astype(bf16)
-            sjv[ROWS * t : ROWS * (t + 2), 128:256] = jnp.concatenate([c0[24:48], c1[24:48]], axis=0).astype(bf16)
-
-            def both(tile, last):
-                turned = pltpu.roll(tile, RANK, 1)
-                return [jnp.where(low_lanes, tile, turned), jnp.where(low_lanes, turned, tile), last]
-
-            rows = jnp.concatenate(
-                both(pra[t, 0:8], pra[t, 8:16]) + both(pra[t + 1, 0:8], pra[t + 1, 8:16]), axis=0
-            )
-            high = rows.astype(bf16).astype(f32)
-            lanes = lax.broadcasted_iota(jnp.int32, rows.shape, 1) < RANK
-            lv[ROWS * t : ROWS * (t + 2), :] = jnp.where(lanes, high, rows - high).astype(bf16)
-        o = dot(lv[...], sjv[...], 0, 0)
-        o = o[0:RANK] + o[RANK:]
+        lanes = lax.broadcasted_iota(jnp.int32, (2 * ROWS, 128), 1) < RANK
+        o = []
+        for h in range(2):
+            for i in range(0, PEERS, 2):
+
+                def three(n):
+                    t = n if h == 0 else n % LINE * LINE + n // LINE
+                    tile = pra[t, 0:8]
+                    turned = pltpu.roll(tile, RANK, 1)
+                    return [jnp.where(low_lanes, tile, turned), jnp.where(low_lanes, turned, tile), pra[t, 8:16]]
+
+                rows = jnp.concatenate(three(i) + three(i + 1), axis=0)
+                high = rows.astype(bf16).astype(f32)
+                lv[ROWS * i : ROWS * (i + 2), :] = jnp.where(lanes, high, rows - high).astype(bf16)
+            both = dot(lv[...], jrecv[h].reshape(TOK, 128), 0, 0)
+            o.append(both[0:RANK] + both[RANK:])
         for p in range(GROUP):
-            opart[p] = o[8 * (p // 2) : 8 * (p // 2) + 8, 128 * (p % 2) : 128 * (p % 2) + 128]
+            opart[p] = o[p % 2][8 * (p // 2) : 8 * (p // 2) + 8]
         orecv[me_d] = opart[me_d]
         to_group(O_RS, lambda p: opart.at[p], orecv.at[me_d])
 
     def sum_out_grad():
         got(O_RS, orecv.at[fifteen])
-        mine = pl.ds(pl.multiple_of(me_t * COLS + core * 128, 128), 128)
+        mine = pl.ds(pl.multiple_of(core * HALF + me_t * 128, 128), 128)
         oz[z] = 2.0 * sum_of(orecv, GROUP) * scale_v[:, mine]
 
         @pl.loop(1, DEPTH)
@@ -439,7 +453,7 @@
         other.wait_recv()
         for t in range(PEERS):
             for c in range(2):
-                at = COLS * t + 128 * c
+                at = HALF * c + 128 * t
                 gout_v[:, at : at + 128] = ob[c, t].astype(f32)
         outs[3].start()
 
@@ -447,38 +461,41 @@
         got(M_AG, gmag_v.at[:, fifteen_cols])
         outs[4].start()
 
-    start_adjust()
-    adjust(0)
-
     pl.semaphore_wait(barrier, PEERS + GROUP - 2)
     for h in range(2):
         go(h, 0, 0, None, slot(h, 1, 0), 0)
         go(h, 0, 0, None, slot(h, -1, 0), 1)
-    pl.loop(1, 5)(adjust)
-    for h in range(2):
-        send_across(h, 0)
-    pl.loop(5, NWB)(adjust)
+    square_part()
     send_squares()
     gate_and_up()
     project()
+    for h in range(2):
+        send_across(h, 0)
+    pl.loop(0, NWB)(adjust)
+    first_along()
+    for h in range(2):
+        send_across(h, 1)
     pl.loop(0, 5)(produce)
-    first_along()
+    sum_squares()
+    sum_projected()
+    for h in range(2):
+        send_across(h, 2)
+    pl.loop(5, 10)(produce)
+    last_along()
     send_columns()
-    pl.loop(5, 8)(produce)
-    sum_squares()
+    for h in range(2):
+        send_across(h, 3)
     for h in range(2):
         forward_across(h, 0)
-    sum_projected()
-    last_along()
-    pl.loop(8, 16)(produce)
+    pl.loop(10, 16)(produce)
+    column_scale()
+    send_rank()
     for h in range(2):
         forward_across(h, 1)
         forward_across(h, 2)
-    column_scale()
-    send_rank()
-    out_grad()
     magacc[...] = jnp.zeros_like(magacc)
     prepare(1)
+    out_grad()
     for h in range(2):
         forward_across(h, 3)
     prepare(0)
@@ -489,12 +506,13 @@
             last_across(h, j)
     prepare(3)
     send_mag()
+    multiply(0)
     sum_out_grad()
-    multiply(0)
+    multiply(1, 0, 512)
     sum_mag_plane()
+    sum_in_grad()
+    multiply(1, 512, F)
     spread_out_grad()
-    sum_in_grad()
-    multiply(1)
     large_grads()
     sum_mag_group()
     swap_out_grad()
@@ -505,8 +523,8 @@
     for c in sent:
         c.wait_send()
     other.wait_send()
-    left_here(J, jsend.at[fifteen])
-    left_here(SQ_RS, sqp.at[:, fifteen_cols])
+    left_here(J, jsend.at[:, pl.ds(0, LINE - 1)])
+    left_here(SQ_RS, sqr.at[fifteen])
     left_here(SQ_AG, sqf.at[:, fifteen_cols])
     left_here(PR_RS, prs.at[fifteen])
     left_here(PR_AG, pra.at[fifteen])
@@ -543,9 +561,9 @@
         V((TOK, F), f32), V((TOK, F), f32), V((ROWS, D), bf16),
         V((2 * RANK, F), bf16), V((2 * RANK, D), bf16), V((1, D), f32), V((F, RANK), bf16),
         V((2, PEERS, 48, QUART), bf16), V((2, TOK, HALF), bf16), V((TOK, D), f32), V((TOK, F), f32),
-        V((8, D), f32), V((8, D), f32), V((1, D), f32), V((1, D), f32),
-        V((PEERS, 48, 128), bf16), V((PEERS, 48, 128), bf16), V((TOK, COLS), bf16),
-        V((1, D), f32), V((PEERS, 1, COLS), f32), V((1, D), f32),
+        V((8, D), f32), V((1, D), f32), V((1, D), f32),
+        V((2, LINE, 96, 128), bf16), V((2, LINE, 96, 128), bf16),
+        V((F, COLS), bf16), V((PEERS, 1, COLS), f32), V((1, D), f32),
         V((PEERS, 16, 128), f32), V((PEERS, 16, 128), f32), V((PEERS, 16, 128), f32),
         V((16, 128), bf16), V((PEERS, 16, 128), bf16), V((TOK, 128), bf16),
         V((GROUP, 16, 256), bf16), V((GROUP, 16, 256), bf16), V((16, 256), bf16), V((GROUP, 16, 256), bf16),
@@ -553,7 +571,7 @@
         V((2, PEERS, RANK, 128), bf16), V((RANK, D), f32),
         V((1, D), f32), V((PEERS, 1, COLS), f32), V((GROUP, 1, COLS), f32), V((1, D), f32),
         V((TOK, F), bf16), V((TOK, F), bf16),
-        pltpu.SemaphoreType.DMA((8,)), pltpu.SemaphoreType.DMA((NWB,)), pltpu.SemaphoreType.DMA((5,)),
+        pltpu.SemaphoreType.DMA((9,)), pltpu.SemaphoreType.DMA((NWB,)), pltpu.SemaphoreType.DMA((5,)),
         pltpu.SemaphoreType.DMA((N_PHASES,)), pltpu.SemaphoreType.DMA((N_PHASES,)),
         pltpu.SemaphoreType.DMA((40,)), pltpu.SemaphoreType.DMA((40,)),
     ]

time: 55.4 us -> 53.3 us (0.962)
  Pallas kernels: 54.7 us -> 52.6 us
    pallas_call x1, Pallas kernels: 51.9 us -> 49.8 us  [on_device(): pl.pallas_call(kernel, out_shape=(jax.ShapeDtypeStruct((TOK, F), bf16), j...]
where the time goes in v3:
time: 53.3 us; the launch traced here: 53.2 us
  Pallas kernels  52.6 us (99%)
  between operations  0.64 us (1%)
    pallas_call x1, Pallas kernels, on_device(): pl.pallas_call(kernel, out_shape=(jax.ShapeDtypeStruct((TOK, F), bf16), j...  49.8 us
    pallas_call x1, Pallas kernels, on_device(): pl.pallas_call(hand_over, out_shape=[jax.ShapeDtypeStruct(o.shape, o.dtyp...  2.77 us

profile of v3, /device:TPU:1, one launch (start us, length us, event | category | flops | bytes accessed | tf_op | source)
XLA Modules:
  0.0 53.2 jit_solution(13440799039432138917)
XLA Ops:
  0.6 49.8 %shard_map.110 = (bf16[384,896]{1,0:T(8,128)(2,1)}, bf16[384,896]{1,0:T(8,128)(2,1)}, f32[64,896]{1,0:T(8,128)}, f32[64,4096]{1,0:T(8,128)}, f32[1,4096]{1,0:T(1,128)}) custom-call(bf16[384,896]{1,0:T(8,128)(2,1)} %gate_h.1, bf16[384,896]{1,0:T(8,128)(2,1)} %up_h.1, bf16[24,4096]{1,0:T(8,128)(2,1)} %cot_h.1, bf16[896,4096]{1,0:T(8,128)(2,1)} %w_h.1, ...), custom_call_target="tpu_custom_call" | custom-call | flops 7000000000 | bytes 14000000 | tf_op jit(solution)/shard_map/pallas_call | solution.py:579
  50.5 2.8 %shard_map.111 = (bf16[384,896]{1,0:T(8,128)(2,1)}, bf16[384,896]{1,0:T(8,128)(2,1)}, f32[64,896]{1,0:T(8,128)}, f32[64,4096]{1,0:T(8,128)}, f32[1,4096]{1,0:T(1,128)}) custom-call(bf16[384,896]{1,0:T(8,128)(2,1)} %get-tuple-element.15.refs_0_, bf16[384,896]{1,0:T(8,128)(2,1)} %get-tuple-element.16.refs_1_, f32[64,896]{1,0:T(8,128)} %get-tuple-element.17.refs_2_, ...), custom_call_target="tpu_custom_call" | custom-call | tf_op jit(solution)/shard_map/pallas_call | solution.py:596

commit v4 on v3

--- a/solution.py
+++ b/solution.py
@@ -25,8 +25,8 @@
 WBLK = 128
 NWB = F // WBLK
 
-(J, SQ_RS, SQ_AG, PR_RS, PR_AG, RC_AG, IN_RS, IN_AG, O_RS, O_PL, O_Z, O_CORE, M_RS, M_DP, M_AG) = range(15)
-N_PHASES = 15
+(J, SQ_RS, SQ_AG, PR_RS, PR_AG, RC_AG, IN_RS, IN_AG, O_RS, O_PL, O_Z, O_CORE, M_RS, M_DP, M_AG, IN_CORE) = range(16)
+N_PHASES = 16
 
 
 def dot(a, b, da, db):
@@ -39,7 +39,7 @@
     w_v, gate_v, up_v, hid_v, u_v, v_v, cot_v, ain_v, aout_v, mag_v, aint_v,
     cotb, scaled, prod, hg, magacc, scale_v, norm_v,
     jsend, jrecv, wj_v, sqr, sqf, prs, prr, pra, rcs, rca, lv,
-    ipart, irecv, isum, iag, gin_v, opart, orecv, oz, ob, gout_v,
+    ipart, irecv, iag, gin_v, opart, orecv, oz, ob, gout_v,
     magp, magr, magd, gmag_v, out_a, out_b,
     loc_sem, w_sem, out_sem, ph_send, ph_recv, g_send, g_recv,
 ):
@@ -49,6 +49,16 @@
     y = lax.div(me_t, LINE)
     z = lax.div(me_d, 2)
     core = lax.rem(me_d, 2)
+
+    barrier = pltpu.get_barrier_semaphore()
+
+    @pl.loop(1, PEERS)
+    def _(d):
+        pl.semaphore_signal(barrier, inc=1, device_id={"tensor": lax.rem(me_t + d, PEERS)}, device_id_type=MESH)
+
+    @pl.loop(1, GROUP)
+    def _(d):
+        pl.semaphore_signal(barrier, inc=1, device_id={"dp": lax.rem(me_d + d, GROUP)}, device_id_type=MESH)
 
     loads = [
         pltpu.make_async_copy(cot_h, cot_v, loc_sem.at[0]),
@@ -77,16 +87,6 @@
     for c in loads[6:]:
         c.start()
 
-    barrier = pltpu.get_barrier_semaphore()
-
-    @pl.loop(1, PEERS)
-    def _(d):
-        pl.semaphore_signal(barrier, inc=1, device_id={"tensor": lax.rem(me_t + d, PEERS)}, device_id_type=MESH)
-
-    @pl.loop(1, GROUP)
-    def _(d):
-        pl.semaphore_signal(barrier, inc=1, device_id={"dp": lax.rem(me_d + d, GROUP)}, device_id_type=MESH)
-
     loads[0].wait()
     for h in range(2):
         left = cot_v[:, HALF * h : HALF * h + QUART].astype(f32)
@@ -156,6 +156,20 @@
 
     def to_group(phase, src, dst):
         exchange(phase, "dp", src, dst, me_d, GROUP)
+
+    def along_z(phase, ref):
+        @pl.loop(1, DEPTH)
+        def _(d):
+            pltpu.make_async_remote_copy(
+                src_ref=ref, dst_ref=ref, send_sem=ph_send.at[phase], recv_sem=ph_recv.at[phase],
+                device_id={"dp": lax.rem(z + d, DEPTH) * 2 + core}, device_id_type=MESH,
+            ).start()
+
+    def swap(phase, ref):
+        return pltpu.make_async_remote_copy(
+            src_ref=ref, dst_ref=ref, send_sem=ph_send.at[phase], recv_sem=ph_recv.at[phase],
+            device_id={"dp": z * 2 + 1 - core}, device_id_type=MESH,
+        )
 
     def my_cols(p):
         return pl.ds(pl.multiple_of(p * COLS, COLS), COLS)
@@ -191,8 +205,8 @@
         part = dot(hid_v[...], ain_v[...], 1, 1)
         for t in range(PEERS):
             r = ROWS * t
-            prs[t, 0:8] = jnp.where(low_lanes, part[r : r + 8], part[r + 8 : r + 16])
-            prs[t, 8:16] = part[r + 16 : r + 24]
+            first = jnp.where(low_lanes, part[r : r + 8], part[r + 8 : r + 16])
+            prs[t] = jnp.concatenate([first, part[r + 16 : r + 24]], axis=0).astype(bf16)
         prr[me_t] = prs[me_t]
         to_plane(PR_RS, lambda p: prs.at[p], prr.at[me_t])
 
@@ -259,7 +273,10 @@
 
     def sum_projected():
         got(PR_RS, prr.at[fifteen])
-        pra[me_t] = sum_of(prr, PEERS)
+        total = prr[0].astype(f32)
+        for t in range(1, PEERS):
+            total = total + prr[t].astype(f32)
+        pra[me_t] = total
         to_plane(PR_AG, lambda p: pra.at[me_t], pra.at[me_t])
 
     def produce(i):
@@ -294,23 +311,14 @@
         got(O_RS, orecv.at[fifteen])
         mine = pl.ds(pl.multiple_of(core * HALF + me_t * 128, 128), 128)
         oz[z] = 2.0 * sum_of(orecv, GROUP) * scale_v[:, mine]
-
-        @pl.loop(1, DEPTH)
-        def _(d):
-            pltpu.make_async_remote_copy(
-                src_ref=oz.at[z], dst_ref=oz.at[z], send_sem=ph_send.at[O_Z], recv_sem=ph_recv.at[O_Z],
-                device_id={"dp": lax.rem(z + d, DEPTH) * 2 + core}, device_id_type=MESH,
-            ).start()
+        along_z(O_Z, oz.at[z])
 
     def spread_out_grad():
         got(O_Z, oz.at[pl.ds(0, DEPTH - 1)])
         ob[core, me_t] = oz[...].reshape(RANK, 128).astype(bf16)
         to_plane(O_PL, lambda p: ob.at[core, me_t], ob.at[core, me_t])
 
-    other = pltpu.make_async_remote_copy(
-        src_ref=ob.at[core], dst_ref=ob.at[core], send_sem=ph_send.at[O_CORE], recv_sem=ph_recv.at[O_CORE],
-        device_id={"dp": z * 2 + 1 - core}, device_id_type=MESH,
-    )
+    other = swap(O_CORE, ob.at[core])
 
     def swap_out_grad():
         got(O_PL, ob.at[0, fifteen])
@@ -358,9 +366,14 @@
         total = irecv[0].astype(f32)
         for t in range(1, GROUP):
             total = total + irecv[t].astype(f32)
-        isum[...] = (2.0 * total).astype(bf16)
-        iag[me_d] = isum[...]
-        to_group(IN_AG, lambda p: isum, iag.at[me_d])
+        iag[core, z] = (2.0 * total).astype(bf16)
+        along_z(IN_AG, iag.at[core, z])
+
+    other_in = swap(IN_CORE, iag.at[core])
+
+    def swap_in_grad():
+        got(IN_AG, iag.at[0, pl.ds(0, DEPTH - 1)])
+        other_in.start()
 
     CH = 256
 
@@ -442,11 +455,11 @@
         outs[1].start()
 
     def finish_in_grad():
-        got(IN_AG, iag.at[fifteen])
+        other_in.wait_recv()
         for b in range(4):
             for g in range(4):
-                w = 256 if g < 3 else 128
-                gin_v[16 * b : 16 * b + 16, 256 * g : 256 * g + w] = iag[4 * b + g, :, 0:w].astype(f32)
+                w, p = 256 if g < 3 else 128, 4 * b + g
+                gin_v[16 * b : 16 * b + 16, 256 * g : 256 * g + w] = iag[p % 2, p // 2, :, 0:w].astype(f32)
         outs[2].start()
 
     def finish_out_grad():
@@ -485,11 +498,11 @@
     send_columns()
     for h in range(2):
         send_across(h, 3)
-    for h in range(2):
-        forward_across(h, 0)
     pl.loop(10, 16)(produce)
     column_scale()
     send_rank()
+    for h in range(2):
+        forward_across(h, 0)
     for h in range(2):
         forward_across(h, 1)
         forward_across(h, 2)
@@ -506,15 +519,16 @@
             last_across(h, j)
     prepare(3)
     send_mag()
+    sum_out_grad()
     multiply(0)
-    sum_out_grad()
-    multiply(1, 0, 512)
+    multiply(1, 0, 256)
     sum_mag_plane()
     sum_in_grad()
-    multiply(1, 512, F)
     spread_out_grad()
+    multiply(1, 256, F)
     large_grads()
     sum_mag_group()
+    swap_in_grad()
     swap_out_grad()
     finish_in_grad()
     finish_out_grad()
@@ -530,7 +544,8 @@
     left_here(PR_AG, pra.at[fifteen])
     left_here(RC_AG, rca.at[fifteen])
     left_here(IN_RS, ipart.at[fifteen])
-    left_here(IN_AG, iag.at[fifteen])
+    left_here(IN_AG, iag.at[0, pl.ds(0, DEPTH - 1)])
+    other_in.wait_send()
     left_here(O_RS, opart.at[fifteen])
     left_here(O_PL, ob.at[0, fifteen])
     left_here(O_Z, oz.at[pl.ds(0, DEPTH - 1)])
@@ -541,17 +556,25 @@
         c.wait()
 
 
+PARTS = (4, 4, 1, 8, 1)
+
+
 def hand_over(*refs):
     src, dst, held, sem_in, sem_out = refs[0:5], refs[5:10], refs[10:15], refs[15], refs[16]
-    into = [pltpu.make_async_copy(src[i], held[i], sem_in.at[i]) for i in range(5)]
-    out = [pltpu.make_async_copy(held[i], dst[i], sem_out.at[i]) for i in range(5)]
+    into, out = [], []
+    for i in range(5):
+        rows = src[i].shape[0] // PARTS[i]
+        for k in range(PARTS[i]):
+            part, n = pl.ds(k * rows, rows), len(into)
+            into.append(pltpu.make_async_copy(src[i].at[part], held[i].at[part], sem_in.at[n]))
+            out.append(pltpu.make_async_copy(held[i].at[part], dst[i].at[part], sem_out.at[n]))
     for c in into:
         c.start()
-    for i in range(5):
-        into[i].wait()
-        out[i].start()
-    for c in out:
+    for c, d in zip(into, out, strict=True):
         c.wait()
+        d.start()
+    for d in out:
+        d.wait()
 
 
 def on_device(gate_act, up_act, cotangent, frozen_weight, adapter_in, adapter_out, magnitude):
@@ -564,9 +587,9 @@
         V((8, D), f32), V((1, D), f32), V((1, D), f32),
         V((2, LINE, 96, 128), bf16), V((2, LINE, 96, 128), bf16),
         V((F, COLS), bf16), V((PEERS, 1, COLS), f32), V((1, D), f32),
-        V((PEERS, 16, 128), f32), V((PEERS, 16, 128), f32), V((PEERS, 16, 128), f32),
+        V((PEERS, 16, 128), bf16), V((PEERS, 16, 128), bf16), V((PEERS, 16, 128), f32),
         V((16, 128), bf16), V((PEERS, 16, 128), bf16), V((TOK, 128), bf16),
-        V((GROUP, 16, 256), bf16), V((GROUP, 16, 256), bf16), V((16, 256), bf16), V((GROUP, 16, 256), bf16),
+        V((GROUP, 16, 256), bf16), V((GROUP, 16, 256), bf16), V((2, DEPTH, 16, 256), bf16),
         V((RANK, F), f32), V((GROUP, 8, 128), f32), V((GROUP, 8, 128), f32), V((DEPTH, 8, 128), f32),
         V((2, PEERS, RANK, 128), bf16), V((RANK, D), f32),
         V((1, D), f32), V((PEERS, 1, COLS), f32), V((GROUP, 1, COLS), f32), V((1, D), f32),
@@ -599,7 +622,7 @@
         in_specs=[hbm] * 5,
         out_specs=[hbm] * 5,
         scratch_shapes=[V(o.shape, o.dtype) for o in outs]
-        + [pltpu.SemaphoreType.DMA((5,)), pltpu.SemaphoreType.DMA((5,))],
+        + [pltpu.SemaphoreType.DMA((sum(PARTS),)), pltpu.SemaphoreType.DMA((sum(PARTS),))],
         compiler_params=pltpu.CompilerParams(vmem_limit_bytes=60 * 1024 * 1024),
     )(*outs)
     return outs[0], outs[1], outs[2], outs[3], outs[4].reshape(D)

time: 53.3 us -> 51.8 us (0.972)
  Pallas kernels: 52.6 us -> 51.1 us
    pallas_call x1, Pallas kernels: 49.8 us -> 48.2 us  [on_device(): pl.pallas_call(kernel, out_shape=(jax.ShapeDtypeStruct((TOK, F), bf16), j...]
where the time goes in v4:
time: 51.8 us; the launch traced here: 51.7 us
  Pallas kernels  51.1 us (99%)
  between operations  0.64 us (1%)
    pallas_call x1, Pallas kernels, on_device(): pl.pallas_call(kernel, out_shape=(jax.ShapeDtypeStruct((TOK, F), bf16), j...  48.2 us
    pallas_call x1, Pallas kernels, on_device(): pl.pallas_call(hand_over, out_shape=[jax.ShapeDtypeStruct(o.shape, o.dtyp...  2.84 us

profile of v4, /device:TPU:1, one launch (start us, length us, event | category | flops | bytes accessed | tf_op | source)
XLA Modules:
  0.0 51.7 jit_solution(6283473782207634940)
XLA Ops:
  0.6 48.2 %shard_map.110 = (bf16[384,896]{1,0:T(8,128)(2,1)}, bf16[384,896]{1,0:T(8,128)(2,1)}, f32[64,896]{1,0:T(8,128)}, f32[64,4096]{1,0:T(8,128)}, f32[1,4096]{1,0:T(1,128)}) custom-call(bf16[384,896]{1,0:T(8,128)(2,1)} %gate_h.1, bf16[384,896]{1,0:T(8,128)(2,1)} %up_h.1, bf16[24,4096]{1,0:T(8,128)(2,1)} %cot_h.1, bf16[896,4096]{1,0:T(8,128)(2,1)} %w_h.1, ...), custom_call_target="tpu_custom_call" | custom-call | flops 7000000000 | bytes 14000000 | tf_op jit(solution)/shard_map/pallas_call | solution.py:602
  48.9 2.8 %shard_map.111 = (bf16[384,896]{1,0:T(8,128)(2,1)}, bf16[384,896]{1,0:T(8,128)(2,1)}, f32[64,896]{1,0:T(8,128)}, f32[64,4096]{1,0:T(8,128)}, f32[1,4096]{1,0:T(1,128)}) custom-call(bf16[384,896]{1,0:T(8,128)(2,1)} %get-tuple-element.15.refs_0_, bf16[384,896]{1,0:T(8,128)(2,1)} %get-tuple-element.16.refs_1_, f32[64,896]{1,0:T(8,128)} %get-tuple-element.17.refs_2_, ...), custom_call_target="tpu_custom_call" | custom-call | tf_op jit(solution)/shard_map/pallas_call | solution.py:619

commit v5 on v4

--- a/solution.py
+++ b/solution.py
@@ -25,7 +25,7 @@
 WBLK = 128
 NWB = F // WBLK
 
-(J, SQ_RS, SQ_AG, PR_RS, PR_AG, RC_AG, IN_RS, IN_AG, O_RS, O_PL, O_Z, O_CORE, M_RS, M_DP, M_AG, IN_CORE) = range(16)
+(O_LINE, SQ_RS, SQ_AG, PR_RS, PR_AG, RC_AG, IN_RS, IN_AG, O_RS, O_PL, O_Z, O_CORE, M_RS, M_DP, M_AG, IN_CORE) = range(16)
 N_PHASES = 16
 
 
@@ -38,7 +38,7 @@
     ggate_h, gup_h, gin_h, gout_h, gmag_h,
     w_v, gate_v, up_v, hid_v, u_v, v_v, cot_v, ain_v, aout_v, mag_v, aint_v,
     cotb, scaled, prod, hg, magacc, scale_v, norm_v,
-    jsend, jrecv, wj_v, sqr, sqf, prs, prr, pra, rcs, rca, lv,
+    oline_s, oline_r, wj_v, sqr, sqf, prs, prr, pra, rcs, rca, lv,
     ipart, irecv, iag, gin_v, opart, orecv, oz, ob, gout_v,
     magp, magr, magd, gmag_v, out_a, out_b,
     loc_sem, w_sem, out_sem, ph_send, ph_recv, g_send, g_recv,
@@ -239,26 +239,6 @@
             a = w_v[rows, cols].astype(f32) + dot(lhs, aout_v[0:RANK, cols], 1, 0)
             w_v[rows, cols] = a.astype(bf16)
 
-    def send_columns():
-        for h in range(2):
-            for d in range(LINE):
-                to = slot(h, 0, d)
-                low = to < PEERS // 2
-                at = pl.ds(pl.multiple_of(lax.rem(to, PEERS // 2) * 128, 128), 128)
-                rows = []
-                for m in range(LINE):
-                    c = cotb[h, y * LINE + m if h == 0 else m * LINE + x, :, at].astype(f32)
-                    rows.append(jnp.where(low, c[0:ROWS], c[ROWS : 2 * ROWS]))
-                jsend[h, d] = jnp.concatenate(rows, axis=0).astype(bf16)
-        for h in range(2):
-            me = y if h == 0 else x
-            jrecv[h, me] = jsend[h, 0]
-            for d in range(1, LINE):
-                pltpu.make_async_remote_copy(
-                    src_ref=jsend.at[h, d], dst_ref=jrecv.at[h, me], send_sem=ph_send.at[J], recv_sem=ph_recv.at[J],
-                    device_id={"tensor": slot(h, 0, d)}, device_id_type=MESH,
-                ).start()
-
     def first_along():
         for h in range(2):
             arrive(h, -1, 0, None, 0)
@@ -276,41 +256,67 @@
         total = prr[0].astype(f32)
         for t in range(1, PEERS):
             total = total + prr[t].astype(f32)
-        pra[me_t] = total
-        to_plane(PR_AG, lambda p: pra.at[me_t], pra.at[me_t])
+        pra[0, x] = total
+        pra[1, y] = total
+        for d in range(1, LINE):
+            for h, own in ((0, x), (1, y)):
+                pltpu.make_async_remote_copy(
+                    src_ref=pra.at[h, own], dst_ref=pra.at[h, own],
+                    send_sem=ph_send.at[PR_AG], recv_sem=ph_recv.at[PR_AG],
+                    device_id={"tensor": slot(h, d, 0)}, device_id_type=MESH,
+                ).start()
 
     def produce(i):
         cols = pl.ds(pl.multiple_of(i * 256, 256), 256)
         prod[:, cols] = dot(hid_v[...], w_v[:, cols], 1, 0)
 
     def out_grad():
-        got(J, jrecv.at[:, pl.ds(0, LINE - 1)])
-        got(PR_AG, pra.at[fifteen])
-        lanes = lax.broadcasted_iota(jnp.int32, (2 * ROWS, 128), 1) < RANK
-        o = []
+        got(PR_AG, pra.at[:, pl.ds(0, LINE - 1)])
+        lanes = lax.broadcasted_iota(jnp.int32, (LINE * ROWS, 128), 1) < RANK
         for h in range(2):
-            for i in range(0, PEERS, 2):
-
-                def three(n):
-                    t = n if h == 0 else n % LINE * LINE + n // LINE
-                    tile = pra[t, 0:8]
-                    turned = pltpu.roll(tile, RANK, 1)
-                    return [jnp.where(low_lanes, tile, turned), jnp.where(low_lanes, turned, tile), pra[t, 8:16]]
-
-                rows = jnp.concatenate(three(i) + three(i + 1), axis=0)
-                high = rows.astype(bf16).astype(f32)
-                lv[ROWS * i : ROWS * (i + 2), :] = jnp.where(lanes, high, rows - high).astype(bf16)
-            both = dot(lv[...], jrecv[h].reshape(TOK, 128), 0, 0)
-            o.append(both[0:RANK] + both[RANK:])
-        for p in range(GROUP):
-            opart[p] = o[p % 2][8 * (p // 2) : 8 * (p // 2) + 8]
+            quarter = x if h == 0 else y
+            at = pl.ds(pl.multiple_of(lax.rem(quarter, 2) * 512, 512), 512)
+            left, right = [], []
+            for m in range(LINE):
+                c = cotb[h, y * LINE + m if h == 0 else m * LINE + x, :, at].astype(f32)
+                right.append(jnp.where(quarter < 2, c[0:ROWS], c[ROWS : 2 * ROWS]))
+                tile = pra[h, m, 0:8]
+                turned = pltpu.roll(tile, RANK, 1)
+                left += [jnp.where(low_lanes, tile, turned), jnp.where(low_lanes, turned, tile), pra[h, m, 8:16]]
+            left = jnp.concatenate(left, axis=0)
+            high = left.astype(bf16).astype(f32)
+            left = jnp.where(lanes, high, left - high).astype(bf16)
+            both = dot(left, jnp.concatenate(right, axis=0).astype(bf16), 0, 0)
+            o = both[0:RANK] + both[RANK:]
+            for zz in range(DEPTH):
+                rows = o[8 * zz : 8 * zz + 8]
+                opart[2 * zz + h] = jnp.concatenate([rows[:, 0:256], rows[:, 256:512]], axis=0).astype(bf16)
         orecv[me_d] = opart[me_d]
         to_group(O_RS, lambda p: opart.at[p], orecv.at[me_d])
 
+    in_line = (1 - core) * y + core * x
+    off_line = (1 - core) * x + core * y
+
     def sum_out_grad():
         got(O_RS, orecv.at[fifteen])
-        mine = pl.ds(pl.multiple_of(core * HALF + me_t * 128, 128), 128)
-        oz[z] = 2.0 * sum_of(orecv, GROUP) * scale_v[:, mine]
+        total = orecv[0].astype(f32)
+        for t in range(1, GROUP):
+            total = total + orecv[t].astype(f32)
+        for j in range(LINE):
+            oline_s[j] = total[8 * (j // 2) : 8 * (j // 2) + 8, 128 * (j % 2) : 128 * (j % 2) + 128]
+        oline_r[in_line] = oline_s[in_line]
+        for d in range(1, LINE):
+            to = lax.rem(in_line + d, LINE)
+            pltpu.make_async_remote_copy(
+                src_ref=oline_s.at[to], dst_ref=oline_r.at[in_line],
+                send_sem=ph_send.at[O_LINE], recv_sem=ph_recv.at[O_LINE],
+                device_id={"tensor": (1 - core) * (to * LINE + x) + core * (y * LINE + to)}, device_id_type=MESH,
+            ).start()
+
+    def sum_out_line():
+        got(O_LINE, oline_r.at[pl.ds(0, LINE - 1)])
+        mine = pl.ds(pl.multiple_of(core * HALF + off_line * 512 + in_line * 128, 128), 128)
+        oz[z] = 2.0 * sum_of(oline_r, LINE) * scale_v[:, mine]
         along_z(O_Z, oz.at[z])
 
     def spread_out_grad():
@@ -406,19 +412,28 @@
                         m = a * prod[rows_of(s0), cols] + b * prod[rows_of(s1), cols]
                         magacc[:, cols] += jnp.sum(m.reshape(ROWS // 8, 8, CH), axis=0)
 
-    def multiply(h, first=0, last=F):
-        for f in range(first, last, 256):
-            w = min(256, F - f)
-            r = dot(scaled[h], w_v[f : f + w, HALF * h : HALF * (h + 1)], 1, 1)
+    def multiply(h, first, last):
+        def block(f, w):
+            units = pl.ds(pl.multiple_of(f, 128), w)
+            r = dot(scaled[h], w_v[units, HALF * h : HALF * (h + 1)], 1, 1)
             for k in range(LINE):
-                block = r[96 * k : 96 * (k + 1)]
+                rows = r[96 * k : 96 * (k + 1)]
                 if h == 0:
                     at = pl.multiple_of(lax.rem(y + k + 3, LINE) * 96, 96)
-                    hg[pl.ds(at, 96), f : f + w] = block
+                    hg[pl.ds(at, 96), units] = rows
                 else:
                     for yy in range(LINE):
                         s = yy * LINE + lax.rem(x + k + 3, LINE)
-                        hg[rows_of(s), f : f + w] += block[ROWS * yy : ROWS * (yy + 1)]
+                        hg[rows_of(s), units] += rows[ROWS * yy : ROWS * (yy + 1)]
+
+        if first < 3:
+
+            @pl.loop(first, min(last, 3))
+            def _(i):
+                block(i * 256, 256)
+
+        if last == 4:
+            block(768, 128)
 
     def send_mag():
         magp[...] = jnp.sum(magacc[...], axis=0, keepdims=True)
@@ -466,7 +481,8 @@
         other.wait_recv()
         for t in range(PEERS):
             for c in range(2):
-                at = HALF * c + 128 * t
+                xx, yy = t % LINE, t // LINE
+                at = HALF + 512 * yy + 128 * xx if c else 512 * xx + 128 * yy
                 gout_v[:, at : at + 128] = ob[c, t].astype(f32)
         outs[3].start()
 
@@ -495,10 +511,11 @@
         send_across(h, 2)
     pl.loop(5, 10)(produce)
     last_along()
-    send_columns()
     for h in range(2):
         send_across(h, 3)
-    pl.loop(10, 16)(produce)
+    pl.loop(10, 13)(produce)
+    out_grad()
+    pl.loop(13, 16)(produce)
     column_scale()
     send_rank()
     for h in range(2):
@@ -508,24 +525,25 @@
         forward_across(h, 2)
     magacc[...] = jnp.zeros_like(magacc)
     prepare(1)
-    out_grad()
     for h in range(2):
         forward_across(h, 3)
     prepare(0)
     prepare(2)
+    sum_out_grad()
     in_grad()
     for h in range(2):
         for j in range(4):
             last_across(h, j)
     prepare(3)
     send_mag()
-    sum_out_grad()
-    multiply(0)
-    multiply(1, 0, 256)
+    multiply(0, 0, 3)
+    sum_out_line()
+    multiply(0, 3, 4)
+    multiply(1, 0, 1)
     sum_mag_plane()
     sum_in_grad()
     spread_out_grad()
-    multiply(1, 256, F)
+    multiply(1, 1, 4)
     large_grads()
     sum_mag_group()
     swap_in_grad()
@@ -537,11 +555,11 @@
     for c in sent:
         c.wait_send()
     other.wait_send()
-    left_here(J, jsend.at[:, pl.ds(0, LINE - 1)])
+    left_here(O_LINE, oline_s.at[pl.ds(0, LINE - 1)])
     left_here(SQ_RS, sqr.at[fifteen])
     left_here(SQ_AG, sqf.at[:, fifteen_cols])
     left_here(PR_RS, prs.at[fifteen])
-    left_here(PR_AG, pra.at[fifteen])
+    left_here(PR_AG, pra.at[:, pl.ds(0, LINE - 1)])
     left_here(RC_AG, rca.at[fifteen])
     left_here(IN_RS, ipart.at[fifteen])
     left_here(IN_AG, iag.at[0, pl.ds(0, DEPTH - 1)])
@@ -585,12 +603,12 @@
         V((2 * RANK, F), bf16), V((2 * RANK, D), bf16), V((1, D), f32), V((F, RANK), bf16),
         V((2, PEERS, 48, QUART), bf16), V((2, TOK, HALF), bf16), V((TOK, D), f32), V((TOK, F), f32),
         V((8, D), f32), V((1, D), f32), V((1, D), f32),
-        V((2, LINE, 96, 128), bf16), V((2, LINE, 96, 128), bf16),
+        V((LINE, 8, 128), f32), V((LINE, 8, 128), f32),
         V((F, COLS), bf16), V((PEERS, 1, COLS), f32), V((1, D), f32),
-        V((PEERS, 16, 128), bf16), V((PEERS, 16, 128), bf16), V((PEERS, 16, 128), f32),
+        V((PEERS, 16, 128), bf16), V((PEERS, 16, 128), bf16), V((2, LINE, 16, 128), f32),
         V((16, 128), bf16), V((PEERS, 16, 128), bf16), V((TOK, 128), bf16),
         V((GROUP, 16, 256), bf16), V((GROUP, 16, 256), bf16), V((2, DEPTH, 16, 256), bf16),
-        V((RANK, F), f32), V((GROUP, 8, 128), f32), V((GROUP, 8, 128), f32), V((DEPTH, 8, 128), f32),
+        V((RANK, F), f32), V((GROUP, 16, 256), bf16), V((GROUP, 16, 256), bf16), V((DEPTH, 8, 128), f32),
         V((2, PEERS, RANK, 128), bf16), V((RANK, D), f32),
         V((1, D), f32), V((PEERS, 1, COLS), f32), V((GROUP, 1, COLS), f32), V((1, D), f32),
         V((TOK, F), bf16), V((TOK, F), bf16),

time: 51.8 us -> 50.9 us (0.983)
  Pallas kernels: 51.1 us -> 50.1 us
    pallas_call x1, Pallas kernels: 48.2 us -> 47.3 us  [on_device(): pl.pallas_call(kernel, out_shape=(jax.ShapeDtypeStruct((TOK, F), bf16), j...]
where the time goes in v5:
time: 50.9 us; the launch traced here: 50.7 us
  Pallas kernels  50.1 us (98%)
  between operations  0.64 us (1%)
    pallas_call x1, Pallas kernels, on_device(): pl.pallas_call(kernel, out_shape=(jax.ShapeDtypeStruct((TOK, F), bf16), j...  47.3 us
    pallas_call x1, Pallas kernels, on_device(): pl.pallas_call(hand_over, out_shape=[jax.ShapeDtypeStruct(o.shape, o.dtyp...  2.84 us

profile of v5, /device:TPU:1, one launch (start us, length us, event | category | flops | bytes accessed | tf_op | source)
XLA Modules:
  0.0 50.7 jit_solution(12901500631906317379)
XLA Ops:
  0.6 47.3 %shard_map.110 = (bf16[384,896]{1,0:T(8,128)(2,1)}, bf16[384,896]{1,0:T(8,128)(2,1)}, f32[64,896]{1,0:T(8,128)}, f32[64,4096]{1,0:T(8,128)}, f32[1,4096]{1,0:T(1,128)}) custom-call(bf16[384,896]{1,0:T(8,128)(2,1)} %gate_h.1, bf16[384,896]{1,0:T(8,128)(2,1)} %up_h.1, bf16[24,4096]{1,0:T(8,128)(2,1)} %cot_h.1, bf16[896,4096]{1,0:T(8,128)(2,1)} %w_h.1, ...), custom_call_target="tpu_custom_call" | custom-call | flops 7000000000 | bytes 14000000 | tf_op jit(solution)/shard_map/pallas_call | solution.py:620
  47.9 2.8 %shard_map.111 = (bf16[384,896]{1,0:T(8,128)(2,1)}, bf16[384,896]{1,0:T(8,128)(2,1)}, f32[64,896]{1,0:T(8,128)}, f32[64,4096]{1,0:T(8,128)}, f32[1,4096]{1,0:T(1,128)}) custom-call(bf16[384,896]{1,0:T(8,128)(2,1)} %get-tuple-element.15.refs_0_, bf16[384,896]{1,0:T(8,128)(2,1)} %get-tuple-element.16.refs_1_, f32[64,896]{1,0:T(8,128)} %get-tuple-element.17.refs_2_, ...), custom_call_target="tpu_custom_call" | custom-call | tf_op jit(solution)/shard_map/pallas_call | solution.py:637

commit v6 on v5

--- a/solution.py
+++ b/solution.py
@@ -541,9 +541,9 @@
     multiply(0, 3, 4)
     multiply(1, 0, 1)
     sum_mag_plane()
+    multiply(1, 1, 4)
     sum_in_grad()
     spread_out_grad()
-    multiply(1, 1, 4)
     large_grads()
     sum_mag_group()
     swap_in_grad()

time: 50.9 us -> 52 us (1.022)
  Pallas kernels: 50.1 us -> 51.3 us
    pallas_call x1, Pallas kernels: 47.3 us -> 48.4 us  [on_device(): pl.pallas_call(kernel, out_shape=(jax.ShapeDtypeStruct((TOK, F), bf16), j...]
where the time goes in v6:
time: 52 us; the launch traced here: 51.9 us
  Pallas kernels  51.3 us (99%)
  between operations  0.64 us (1%)
    pallas_call x1, Pallas kernels, on_device(): pl.pallas_call(kernel, out_shape=(jax.ShapeDtypeStruct((TOK, F), bf16), j...  48.4 us
    pallas_call x1, Pallas kernels, on_device(): pl.pallas_call(hand_over, out_shape=[jax.ShapeDtypeStruct(o.shape, o.dtyp...  2.84 us

profile of v6, /device:TPU:1, one launch (start us, length us, event | category | flops | bytes accessed | tf_op | source)
XLA Modules:
  0.0 51.9 jit_solution(8145196597527673480)
XLA Ops:
  0.6 48.4 %shard_map.110 = (bf16[384,896]{1,0:T(8,128)(2,1)}, bf16[384,896]{1,0:T(8,128)(2,1)}, f32[64,896]{1,0:T(8,128)}, f32[64,4096]{1,0:T(8,128)}, f32[1,4096]{1,0:T(1,128)}) custom-call(bf16[384,896]{1,0:T(8,128)(2,1)} %gate_h.1, bf16[384,896]{1,0:T(8,128)(2,1)} %up_h.1, bf16[24,4096]{1,0:T(8,128)(2,1)} %cot_h.1, bf16[896,4096]{1,0:T(8,128)(2,1)} %w_h.1, ...), custom_call_target="tpu_custom_call" | custom-call | flops 7000000000 | bytes 14000000 | tf_op jit(solution)/shard_map/pallas_call | solution.py:620
  49.1 2.8 %shard_map.111 = (bf16[384,896]{1,0:T(8,128)(2,1)}, bf16[384,896]{1,0:T(8,128)(2,1)}, f32[64,896]{1,0:T(8,128)}, f32[64,4096]{1,0:T(8,128)}, f32[1,4096]{1,0:T(1,128)}) custom-call(bf16[384,896]{1,0:T(8,128)(2,1)} %get-tuple-element.15.refs_0_, bf16[384,896]{1,0:T(8,128)(2,1)} %get-tuple-element.16.refs_1_, f32[64,896]{1,0:T(8,128)} %get-tuple-element.17.refs_2_, ...), custom_call_target="tpu_custom_call" | custom-call | tf_op jit(solution)/shard_map/pallas_call | solution.py:637
